TPU v7x, 128 devices: a whole 4x4x4 slice. The times are simulated.
128 devices in a mesh: grp: 16 (over z, y_hi, core), blk: 8 (over y_lo, x).
Axes of the slice: x: 4, y: 4 (y_hi: 2, y_lo: 2; y = y_hi * 2 + y_lo), z: 4, core: 2. Of those that a mesh axis runs over, the one named last changes fastest.
Arguments:
- embed: bfloat16 [65536, 1024], P(('grp', 'blk')), may hold values from -6 to 6
- owner: int32 [65536, 1], P(('grp', 'blk')), may hold values from 0 to 15; in each aligned block of 512 rows (0 to 511, 512 to 1023, ...) at most 64 rows name the same one
- local_id: int32 [65536], P(('grp', 'blk')), may hold values from 0 to 127
- rank: int32 [65536], P(('grp', 'blk')), may hold values from 0 to 65535, each once
Outputs:
- highest: float32 [65536], P(('grp', 'blk'))
Inputs may be any that keep to these rules, and one draw needn't show every extreme that they name: `owner`: among the 512 rows of one device, at most 64 name one group. `rank`: every value appears exactly once.
All inputs are finite; a program needn't handle non-finite values.
Results may differ from a plain program's by a relative error of at most 0.00068.
Values may be sent and summed in bfloat16 or wider, within the bound.
No kernel may reach another device: no remote copies, remote signals or barrier semaphores. Data moves between devices by JAX's collectives and lax.ppermute only.
A program may use at most 64 MiB of HBM per device.

v0:
```python
import math

import jax
import jax.numpy as jnp
from jax import lax
from jax.sharding import PartitionSpec as P

EPS = 1e-06
BEYOND = 1073741824


def pair_scores(query, query_tag, query_rank, keys, key_tag, key_rank):
    scores = lax.dot_general(
        query, keys, (((1,), (1,)), ((), ())), preferred_element_type=jnp.float32
    )
    same = (
        (query_tag[:, None] == key_tag[None, :])
        & (key_tag[None, :] >= 0)
        & (query_tag[:, None] >= 0)
    )
    row_side = jnp.where(
        same & (key_rank[None, :] < query_rank[:, None]), scores, jnp.float32(-1.0)
    )
    column_side = jnp.where(
        same & (query_rank[:, None] < key_rank[None, :]), scores, jnp.float32(-1.0)
    )
    return (jnp.max(row_side, axis=1), jnp.max(column_side, axis=0))


def tile_split(rows, tags, ranks, tile):
    count = rows.shape[0] // tile
    sort_key = jnp.where(tags >= 0, tags, BEYOND).reshape(count, tile)
    return (
        rows.reshape(count, tile, -1),
        tags.reshape(count, tile),
        ranks.reshape(count, tile),
        jnp.min(sort_key, 1),
        jnp.max(sort_key, 1),
    )


def tiled_scores(query, query_tag, query_rank, keys, key_tag, key_rank):
    tile = math.gcd(query.shape[0], 256)
    query_tiles = tile_split(query, query_tag, query_rank, tile)
    key_tiles = tile_split(keys, key_tag, key_rank, tile)
    empty = jnp.full((tile,), -1.0, jnp.float32)

    def outer(column_carry, query_block):
        q_rows, q_tag, q_rank, q_low, q_high = query_block

        def inner(row_carry, key_block):
            k_rows, k_tag, k_rank, k_low, k_high = key_block
            meet = (q_low <= k_high) & (k_low <= q_high) & (q_low < BEYOND) & (k_low < BEYOND)
            row_best, column_best = lax.cond(
                meet,
                lambda: pair_scores(q_rows, q_tag, q_rank, k_rows, k_tag, k_rank),
                lambda: (empty, empty),
            )
            return (jnp.maximum(row_carry, row_best), column_best)

        row_best, columns = lax.scan(inner, empty, key_tiles)
        return (jnp.maximum(column_carry, columns), row_best)

    start_columns = jnp.full((keys.shape[0] // tile, tile), -1.0, jnp.float32)
    columns, rows = lax.scan(outer, start_columns, query_tiles)
    return (rows.reshape(-1), columns.reshape(-1))


def per_device(embed, owner, local_id, rank):
    n_group = lax.axis_size("grp")
    row_count = embed.shape[0]
    capacity = row_count // 8
    width = n_group * capacity
    wide = embed.astype(jnp.float32)
    unit = (wide * lax.rsqrt(jnp.sum(wide * wide, 1, keepdims=True) + EPS)).astype(jnp.bfloat16)
    target = owner[:, 0]
    onehot = (target[:, None] == jnp.arange(n_group, dtype=jnp.int32)[None, :]).astype(jnp.int32)
    position = jnp.sum((jnp.cumsum(onehot, 0) - 1) * onehot, 1)
    slot_index = target * capacity + position
    send_unit = jnp.zeros((width, unit.shape[1]), jnp.bfloat16).at[slot_index].set(unit)
    send_tag = jnp.full((width,), -1, jnp.int32).at[slot_index].set(local_id)
    send_rank = jnp.zeros((width,), jnp.int32).at[slot_index].set(rank)
    routed, routed_tag, routed_rank = (
        lax.all_to_all(
            send_unit.reshape(n_group, capacity, -1), "grp", split_axis=0, concat_axis=0, tiled=True
        ),
        lax.all_to_all(
            send_tag.reshape(n_group, capacity), "grp", split_axis=0, concat_axis=0, tiled=True
        ),
        lax.all_to_all(
            send_rank.reshape(n_group, capacity), "grp", split_axis=0, concat_axis=0, tiled=True
        ),
    )
    routed_tag = routed_tag.reshape(width)
    ordering = jnp.argsort(jnp.where(routed_tag >= 0, routed_tag, BEYOND), stable=True)
    query = routed.reshape(width, -1)[ordering]
    query_tag = routed_tag[ordering]
    query_rank = routed_rank.reshape(width)[ordering]
    start_best = jnp.full((width,), -1.0, jnp.float32)
    keys = lax.all_gather(query, "blk", axis=0, tiled=True)
    key_tag = lax.all_gather(query_tag, "blk", axis=0, tiled=True)
    key_rank = lax.all_gather(query_rank, "blk", axis=0, tiled=True)
    row_best, unused = tiled_scores(query, query_tag, query_rank, keys, key_tag, key_rank)
    highest = jnp.maximum(start_best, row_best)
    in_slots = jnp.zeros((width,), jnp.float32).at[ordering].set(highest)
    home = lax.all_to_all(
        in_slots.reshape(n_group, capacity), "grp", split_axis=0, concat_axis=0, tiled=True
    )
    return home.reshape(width)[slot_index]


def solution(mesh):
    in_specs = (
        P(("grp", "blk"), None),
        P(("grp", "blk"), None),
        P(("grp", "blk")),
        P(("grp", "blk")),
    )
    out_specs = P(("grp", "blk"))
    return jax.shard_map(
        per_device, mesh=mesh, in_specs=in_specs, out_specs=out_specs, check_vma=False
    )
```

profile of v0, /device:TPU:0, one launch (start us, length us, event | category | flops | bytes accessed | tf_op | source)
XLA Modules:
  0.0 942.5 jit_solution(14307542212418086791)
XLA Ops:
  10.1 2.6 scatter_custom_fusion
  13.4 8.1 all-to-all-start
  21.5 1.5 fusion.5
  23.0 4.9 scatter_custom_fusion.1
  29.1 6.1 all-to-all-start.1
  36.5 4.4 sort.17
  40.8 23.6 %all-to-all-done.1 = bf16[16,64,1024]{2,1,0:T(8,128)(2,1)S(1)} async-done(((bf16[16,64,1024]{2,1,0:T(8,128)(2,1)}), bf16[16,64,1024]{2,1,0:T(8,128)(2,1)S(1)}, u32[]{:S(2)}, u32[]{:S(2)}) %all-to-all-start.1) | async-done | bytes 2097184 | tf_op jit(solution)/shard_map/all_to_all | solution.py:84
  64.4 5.4 gather_fusion.1
  69.8 2.6 scatter_custom_fusion.2
  73.1 3.4 all-to-all-start.2
  76.6 4.5 gather_fusion
  81.1 28.3 %all-gather = s32[8192]{0:T(1024)S(1)} all-gather(s32[1024]{0:T(1024)S(1)} %gather_fusion), channel_id=2, replica_groups=mesh['grp'=16,'blk'=8] {'blk'}, dimensions={0}, use_global_device_ids=true | all-gather | bytes 36864 | tf_op jit(solution)/shard_map/all_gather | solution.py:101
  110.2 4.5 gather_fusion.2
  114.7 28.3 %all-gather.1 = s32[8192]{0:T(1024)S(1)} all-gather(s32[1024]{0:T(1024)S(1)} %gather_fusion.2), channel_id=3, replica_groups=mesh['grp'=16,'blk'=8] {'blk'}, dimensions={0}, use_global_device_ids=true | all-gather | bytes 36864 | tf_op jit(solution)/shard_map/all_gather | solution.py:102
  143.3 95.4 %all-gather.5.cloned.1.call-done = bf16[8192,1024]{1,0:T(8,128)(2,1)} async-done(((bf16[1024,1024]{1,0:T(8,128)(2,1)}), bf16[8192,1024]{1,0:T(8,128)(2,1)}) %all-gather.5.cloned.1.call-update) | async-done | bytes 16777232 | tf_op jit(solution)/shard_map/all_gather | solution.py:100
  238.7 606.5 %while.23 = (s32[]{:T(128)}, f32[4,256]{1,0:T(4,128)S(1)}, s32[4]{0:T(128)S(1)}, s32[4]{0:T(128)S(1)}, bf16[4,256,1024]{2,1,0:T(8,128)(2,1)}, /*index=5*/s32[4,2...) while((s32[]{:T(128)}, f32[4,256]{1,0:T(4,128)S(1)}, ...), condition=%wide.region_18.19_spmd, body=%wide.region_12.18_spmd.sunk | while | flops 134677248 | bytes 2119806 | solution.py:65
  241.6 156.2 %while.24 = (s32[]{:T(128)}, f32[256]{0:T(256)S(1)}, s32[32]{0:T(128)S(1)}, s32[]{:T(128)}, s32[32]{0:T(128)S(1)}, /*index=5*/s32[]{:T(128)}, pred[]{:T(512)}, s...) while((s32[]{:T(128)}, f32[256]{0:T(256)S(1)}, ...), condition=%wide.region_17.17_spmd.clone, body=%wide.region_13.16_spmd.clone.sunk | while | flops 134677248 | bytes 1064740 | solution.py:61
  245.9 1.5 conditional.3
  264.9 1.5 conditional.3
  283.9 1.5 conditional.3
  289.7 1.5 conditional.3
  304.3 1.5 conditional.3
  323.3 1.5 conditional.3
  342.3 1.5 conditional.3
  361.3 1.5 conditional.3
  367.1 1.5 conditional.3
  381.7 1.5 conditional.3
  387.6 1.5 conditional.3
  400.8 157.6 %while.24 = (s32[]{:T(128)}, f32[256]{0:T(256)S(1)}, s32[32]{0:T(128)S(1)}, s32[]{:T(128)}, s32[32]{0:T(128)S(1)}, /*index=5*/s32[]{:T(128)}, pred[]{:T(512)}, s...) while((s32[]{:T(128)}, f32[256]{0:T(256)S(1)}, ...), condition=%wide.region_17.17_spmd.clone, body=%wide.region_13.16_spmd.clone.sunk | while | flops 134677248 | bytes 1064740 | solution.py:61
  409.5 1.5 conditional.3
  424.1 1.5 conditional.3
  430.0 1.5 conditional.3
  448.9 1.5 conditional.3
  449.0 1.4 fusion.1
  463.5 1.5 conditional.3
  469.4 1.5 conditional.3
  484.0 1.5 conditional.3
  489.8 1.5 conditional.3
  504.4 1.5 conditional.3
  510.2 1.5 conditional.3
  529.2 1.5 conditional.3
  548.2 1.5 conditional.3
  561.5 140.3 %while.24 = (s32[]{:T(128)}, f32[256]{0:T(256)S(1)}, s32[32]{0:T(128)S(1)}, s32[]{:T(128)}, s32[32]{0:T(128)S(1)}, /*index=5*/s32[]{:T(128)}, pred[]{:T(512)}, s...) while((s32[]{:T(128)}, f32[256]{0:T(256)S(1)}, ...), condition=%wide.region_17.17_spmd.clone, body=%wide.region_13.16_spmd.clone.sunk | while | flops 134677248 | bytes 1064740 | solution.py:61
  704.8 140.3 %while.24 = (s32[]{:T(128)}, f32[256]{0:T(256)S(1)}, s32[32]{0:T(128)S(1)}, s32[]{:T(128)}, s32[32]{0:T(128)S(1)}, /*index=5*/s32[]{:T(128)}, pred[]{:T(512)}, s...) while((s32[]{:T(128)}, f32[256]{0:T(256)S(1)}, ...), condition=%wide.region_17.17_spmd.clone, body=%wide.region_13.16_spmd.clone.sunk | while | flops 134677248 | bytes 1064740 | solution.py:61
  845.2 4.3 scatter_custom_fusion.3
  850.2 73.4 %all-to-all-start.3 = ((f32[16,1,64]{2,1,0:T(1,128)}), f32[16,1,64]{2,1,0:T(1,128)S(1)}, u32[]{:S(2)}, u32[]{:S(2)}) async-start(f32[16,1,64]{2,1,0:T(1,128)} %all_to_all.26), calls=%async_computation.3 | async-start | bytes 16384 | tf_op jit(solution)/shard_map/all_to_all | solution.py:106
  923.6 7.4 all-to-all-done.3
  932.3 3.4 gather_fusion.3
  (747 shorter events, 210.9 us)
Async XLA Ops:
  13.4 15.7 %all-to-all-start = ((s32[16,1,64]{2,1,0:T(1,128)}), s32[16,1,64]{2,1,0:T(1,128)S(1)}, u32[]{:S(2)}, u32[]{:S(2)}) async-start(s32[16,1,64]{2,1,0:T(1,128)} %all_to_all.21), calls=%async_computation | async-start | bytes 16384 | tf_op jit(solution)/shard_map/all_to_all | solution.py:87
  29.1 35.4 %all-to-all-start.1 = ((bf16[16,64,1024]{2,1,0:T(8,128)(2,1)}), bf16[16,64,1024]{2,1,0:T(8,128)(2,1)S(1)}, u32[]{:S(2)}, u32[]{:S(2)}) async-start(bf16[16,64,1024]{2,1,0:T(8,128)(2,1)} %bitcast.65), calls=%async_computation.1 | async-start | bytes 4194304 | tf_op jit(solution)/shard_map/all_to_all | solution.py:84
  35.1 203.6 %all-gather.5.cloned.1.call-start = ((), (), s32[]{:S(2)}) async-start(), calls=%async_computation.4 | async-start | bytes 18874368 | tf_op jit(solution)/shard_map/all_gather | solution.py:100
  73.1 36.3 %all-to-all-start.2 = ((s32[16,1,64]{2,1,0:T(1,128)}), s32[16,1,64]{2,1,0:T(1,128)S(1)}, u32[]{:S(2)}, u32[]{:S(2)}) async-start(s32[16,1,64]{2,1,0:T(1,128)} %all_to_all.24), calls=%async_computation.2 | async-start | bytes 16384 | tf_op jit(solution)/shard_map/all_to_all | solution.py:90
  850.2 80.8 %all-to-all-start.3 = ((f32[16,1,64]{2,1,0:T(1,128)}), f32[16,1,64]{2,1,0:T(1,128)S(1)}, u32[]{:S(2)}, u32[]{:S(2)}) async-start(f32[16,1,64]{2,1,0:T(1,128)} %all_to_all.26), calls=%async_computation.3 | async-start | bytes 16384 | tf_op jit(solution)/shard_map/all_to_all | solution.py:106
Sparse Core Ops, SparseCore 0:
  69.9 168.7 all-gather.4
where the time goes:
time: 953 us; the launch traced here: 943 us
  loops' own time  407 us (43%)
  local copies, waits for them, and re-layouts  196 us (21%)
  waiting for transfers between devices  128 us (13%)
  starting transfers between devices  91.1 us (10%)
  blocking collectives  56.5 us (6%)
  matrix products  32.4 us (3%)
  other arithmetic  18.2 us (2%)
  between operations  13.6 us (1%)
    another operation x4, loops' own time, outer(): row_best, columns = lax.scan(inner, empty, key_tiles)  401 us
    dynamic_slice x279, local copies, waits for them, and re-layouts, outer(): row_best, columns = lax.scan(inner, empty, key_tiles)  156 us
    all_gather x1, waiting for transfers between devices, per_device(): keys = lax.all_gather(query, 'blk', axis=0, tiled=True)  95.4 us
    all_to_all x1, starting transfers between devices, per_device(): lax.all_to_all(in_slots.reshape(n_group, capacity), 'grp', split_axis=0,...  73.4 us
    dot_general x23, matrix products, pair_scores(): lax.dot_general(query, keys, (((1,), (1,)), ((), ())), preferred_element_...  32.4 us
    all_gather x1, blocking collectives, per_device(): key_rank = lax.all_gather(query_rank, 'blk', axis=0, tiled=True)  28.3 us
    all_gather x1, blocking collectives, per_device(): key_tag = lax.all_gather(query_tag, 'blk', axis=0, tiled=True)  28.3 us
    all_to_all x1, waiting for transfers between devices, per_device(): lax.all_to_all(send_unit.reshape(n_group, capacity, -1), 'grp', split_axi...  23.6 us
  transfers between devices with their start and end apart: 5, of which 4 were waited for; matrix products, arithmetic and copies ran while one was open for 3% of the time, Pallas kernels for 0%

commit v1 on v0

v1 whole, which is shorter than its diff:
```python
import functools

import jax
import jax.numpy as jnp
from jax import lax
from jax.experimental import pallas as pl
from jax.experimental.pallas import tpu as pltpu
from jax.sharding import PartitionSpec as P

EPS = 1e-06
BOTH = ("grp", "blk")
CHIPS = 64
BLOCK = 24
SEATS = 23
EXTRA = 128
CHUNK = 8 * BLOCK
WINDOW = CHUNK + 16
TILE = 256
TILES = 6
PACKED = TILE * TILES
ROOM = PACKED
SPILL = 128
GROUPS = [[g * 8 + b for g in range(core, 16, 2) for b in range(8)] for core in range(2)]
COLS = (((1,), (1,)), ((), ()))
F32 = jnp.float32
BF16 = jnp.bfloat16
I32 = jnp.int32


def iota(shape, dim):
    return lax.broadcasted_iota(I32, shape, dim)


def hot(mask):
    return jnp.where(mask, jnp.float32(1), jnp.float32(0)).astype(BF16)


def dot(a, b, dims=(((1,), (0,)), ((), ()))):
    return lax.dot_general(a, b, dims, preferred_element_type=F32)


def thirds(x):
    high = x.astype(BF16)
    rest = x - high.astype(F32)
    middle = rest.astype(BF16)
    return high, middle, (rest - middle.astype(F32)).astype(BF16)


def fields_of(extra):
    return dot(hot(iota((16, EXTRA), 0) == iota((16, EXTRA), 1)), extra, COLS)


def send_kernel(me, embed, owner, local, rank, out, place, unit, slot, ends):
    rows, width = embed.shape
    step = pl.program_id(0)
    block = out.shape[0]

    @pl.when(step == 0)
    def _():
        wide = embed[...].astype(F32)
        scale = lax.rsqrt(jnp.sum(wide * wide, 1, keepdims=True) + EPS)
        unit[...] = (wide * scale).astype(BF16)
        group, number, order = owner[...], local[...], rank[...]
        chip = (number & (CHIPS - 1)) ^ (group * 4)
        own = iota((CHIPS, rows), 0) == chip
        near = iota((CHIPS, rows), 0) == (chip ^ 1)
        before = hot(iota((rows, rows), 0) < iota((rows, rows), 1))
        ahead = dot(hot(own), before)
        count = jnp.sum(jnp.where(own, 1.0, 0.0), 1, keepdims=True)
        position = jnp.sum(jnp.where(own, ahead, 0.0), 0, keepdims=True).astype(I32)
        beside = jnp.sum(jnp.where(near, count, 0.0), 0, keepdims=True).astype(I32)
        spilled = position >= SEATS
        seat = jnp.where(spilled, beside + position - SEATS, position)
        late = jnp.max(jnp.where(seat >= SEATS, 1.0, 0.0), 1, keepdims=True)
        goes = jnp.where(seat < SEATS, jnp.where(spilled, chip ^ 1, chip), -1)
        line = seat + jnp.where(spilled, 32, 0)
        slot[...] = jnp.where(goes >= 0, goes * BLOCK + seat, -1)
        place[...] = jnp.where(iota(place.shape, 0) == 0, chip, line)
        entries = (
            number,
            group,
            order >> 8,
            order & 255,
            jnp.ones_like(order),
            jnp.where(spilled, 1, 0),
            (line + (me[0] & 7) * BLOCK) & (EXTRA - 1),
            jnp.broadcast_to(me[0], order.shape),
        )
        there = iota((CHIPS, rows), 0) == goes
        tables = [jnp.where(there, entry.astype(F32), 0.0).astype(BF16) for entry in entries]
        seats = hot(iota((EXTRA, rows), 0) == seat)
        fields = dot(jnp.concatenate(tables, 0), seats, COLS)
        lane = iota((CHIPS, EXTRA), 1)
        for at in range(len(entries)):
            field = fields[CHIPS * at : CHIPS * (at + 1), :]
            if at == 0:
                field = jnp.where(lane == EXTRA - 1, late, field)
            ends[:, EXTRA * at : EXTRA * (at + 1)] = field

    pick = hot(iota((block, rows), 0) == slot[...] - step * block)
    moved = dot(pick, unit[...])
    end = ends[pl.ds(pl.multiple_of(step * 8, 8), 8), :]
    last = iota((8, width), 0) == 7
    pieces = []
    for at in range(block // BLOCK):
        top = at * BLOCK
        pieces.append(moved[top : top + 16, :])
        pieces.append(jnp.where(last, end[at : at + 1, :], moved[top + 16 : top + 24, :]))
    out[...] = jnp.concatenate(pieces, 0).astype(BF16)


def gather(spot, count, taken, rows, fields):
    pick = hot(iota((count, CHUNK), 0) == spot)
    return dot(pick, taken[rows, :]), dot(pick, fields, COLS)


def load_chunks(source, taken, copied):
    copies = []
    for at in range(taken.shape[0] // CHUNK):
        rows = pl.ds(at * CHUNK, CHUNK)
        copies.append(pltpu.make_async_copy(source.at[rows, :], taken.at[rows, :], copied.at[at]))
        copies[-1].start()
    return copies


def read_kernel(source, spill, spots, fields, info, taken, pile, strange, copied):
    chunks = taken.shape[0] // CHUNK
    width = taken.shape[1]
    copies = load_chunks(source, taken, copied)
    upto = hot(iota((CHUNK, CHUNK), 0) <= iota((CHUNK, CHUNK), 1))
    ends = hot(iota((16, CHUNK), 1) == iota((16, CHUNK), 0) * BLOCK + SEATS)
    place = iota((EXTRA, CHUNK), 1)
    sender = jnp.zeros(place.shape, I32)
    for at in range(1, 8):
        sender = sender + jnp.where(place >= at * BLOCK, 1, 0)
    spread = hot(place - sender * BLOCK == iota((EXTRA, CHUNK), 0))
    mine = (iota((64, CHUNK), 0) & 7) == sender[:64, :]
    spots[...] = jnp.full(spots.shape, -1, I32)
    start, start_strange = jnp.int32(0), jnp.int32(0)
    late = jnp.zeros((8, 1), F32)
    for at in range(chunks):
        copies[at].wait()
        rows = pl.ds(at * CHUNK, CHUNK)
        lines = dot(ends, taken[rows, :])[:8, :]
        late = jnp.maximum(late, lines[:, EXTRA - 1 : EXTRA])
        stack = [lines[:, EXTRA * f : EXTRA * (f + 1)] for f in range(8)]
        wide = dot(jnp.concatenate(stack, 0).astype(BF16), spread)
        wide = jnp.where(mine, wide, 0.0)
        found = [jnp.sum(wide[8 * f : 8 * f + 8, :], 0, keepdims=True) for f in range(8)]
        table = jnp.concatenate(found + [jnp.zeros((EXTRA - 8, CHUNK), F32)], 0)
        fields[at] = table.astype(BF16)
        foreign = found[5]
        native = found[4] - foreign
        both = jnp.where(iota((16, CHUNK), 0) == 0, native, foreign)
        running = dot(both.astype(BF16), upto).astype(I32)
        spots[at : at + 1, 0:CHUNK] = jnp.where(native > 0, running[0:1, :] + (start - 1), -1)
        strange[at : at + 1, :] = jnp.where(
            foreign > 0, running[1:2, :] + (start_strange - 1), -1
        )
        info[at] = (start >> 4) << 4
        start = start + jnp.sum(native).astype(I32)
        start_strange = start_strange + jnp.sum(foreign).astype(I32)
    full = (start > PACKED) | (start_strange > SPILL) | (jnp.max(late) > 0)
    info[16] = jnp.minimum((start + TILE - 1) // TILE, TILES)
    info[17] = jnp.where(full, 1, 0)
    pile[...] = jnp.zeros(pile.shape, F32)

    @pl.when(start_strange > 0)
    def _():
        def step(at, carry):
            rows = pl.ds(pl.multiple_of(at * CHUNK, CHUNK), CHUNK)
            rows_in, side = gather(strange[pl.ds(at, 1), :], SPILL, taken, rows, fields[at])
            pile[:, :width] += rows_in
            pile[:, width:] += side
            return carry

        lax.fori_loop(0, chunks, step, 0)

    spill[...] = pile[...].astype(BF16)


def pack_kernel(info, source, spots, fields, packed, taken, room, copied, placed):
    chunks = taken.shape[0] // CHUNK
    width = taken.shape[1]
    copies = load_chunks(source, taken, copied)
    tiles = info[16]
    room[0:16, :] = jnp.zeros((16, room.shape[1]), BF16)
    first = jnp.int32(0)
    for at in range(chunks):
        first = pl.multiple_of(jnp.minimum(info[at], ROOM - WINDOW), 16)
        spot = spots[at : at + 1, 0:CHUNK] - first
        copies[at].wait()
        rows_in, side = gather(spot, WINDOW, taken, pl.ds(at * CHUNK, CHUNK), fields[at])
        here = pl.ds(first, 16)
        after = pl.ds(pl.multiple_of(first + 16, 16), WINDOW - 16)
        for span, value in ((pl.ds(0, width), rows_in), (pl.ds(width, EXTRA), side)):
            room[here, span] = (room[here, span].astype(F32) + value[:16]).astype(BF16)
            room[after, span] = value[16:].astype(BF16)

    def clear(at, carry):
        room[pl.ds(pl.multiple_of(at * 16, 16), 16), :] = jnp.zeros((16, room.shape[1]), BF16)
        return carry

    lax.fori_loop((first + WINDOW) // 16, tiles * (TILE // 16), clear, 0)
    for wait in (False, True):
        for at in range(TILES):
            rows = pl.ds(at * TILE, TILE)
            copy = pltpu.make_async_copy(room.at[rows, :], packed.at[rows, :], placed.at[at])
            pl.when(at < tiles)(copy.wait if wait else copy.start)


def score(queries, low, high, keys, key_tiles, best, marks):
    width = queries.shape[1] - EXTRA

    def mark_step(at, carry):
        span = pl.ds(pl.multiple_of(at * TILE, TILE), TILE)
        side = keys[span, width:].astype(F32).astype(I32)
        mark = (side[:, 1:2] * 128 + side[:, 0:1] + side[:, 4:5]) * 65536
        mark = mark + side[:, 2:3] * 256 + side[:, 3:4]
        marks[span, :] = jnp.broadcast_to(mark, (TILE, TILE))
        return carry

    lax.fori_loop(0, key_tiles, mark_step, 0)

    def against(size):
        def query_step(at, carry):
            rows = pl.ds(pl.multiple_of(at * TILE, TILE), TILE)
            fields = fields_of(queries[rows, width:]).astype(I32)
            cluster = (fields[1:2, :] * 128 + fields[0:1, :] + fields[4:5, :]) * 65536
            upper = cluster + fields[2:3, :] * 256 + fields[3:4, :]
            mark = marks[:size, :]
            scores = dot(keys[:size, :width], queries[rows, :width], COLS)
            earlier = (mark >= cluster) & (mark < upper)
            found = jnp.max(jnp.where(earlier, scores, -1.0), 0, keepdims=True)
            best[:, rows] = jnp.maximum(best[:, rows], found)
            return carry

        lax.fori_loop(low, high, query_step, 0)

    if isinstance(key_tiles, int):
        against(key_tiles * TILE)
        return
    for tiles in range(1, keys.shape[0] // TILE + 1):
        pl.when(key_tiles == tiles)(functools.partial(against, tiles * TILE))


def fetch(source, target, tiles, sems):
    for at in range(TILES):
        rows = pl.ds(at * TILE, TILE)
        copy = pltpu.make_async_copy(source.at[rows, :], target.at[rows, :], sems.at[at])
        pl.when(at < tiles)(copy.start)


def fetched(source, target, tiles, sems):
    for at in range(TILES):
        rows = pl.ds(at * TILE, TILE)
        copy = pltpu.make_async_copy(source.at[rows, :], target.at[rows, :], sems.at[at])
        pl.when(at < tiles)(copy.wait)


def own_kernel(info, packed, best, mine, marks, sems):
    fetch(packed, mine, info[16], sems)
    best[...] = jnp.full(best.shape, -1.0, F32)
    fetched(packed, mine, info[16], sems)
    score(mine, 0, info[16], mine, info[16], best, marks)


def other_kernel(
    info, other_info, packed, other, near, cross, best_in, spots, back,
    mine, theirs, best, marks, sems, other_sems,
):
    tiles, other_tiles = info[16], other_info[16]
    width = mine.shape[1] - EXTRA
    fetch(packed, mine, tiles, sems)
    fetch(other, theirs, other_tiles, other_sems)
    best[:, :PACKED] = best_in[...]
    best[:, PACKED:] = jnp.full((1, best.shape[1] - PACKED), -1.0, F32)
    spilled = jnp.max(near[:, width:].astype(F32)[:, 4:5]) + jnp.max(
        cross[:, width:].astype(F32)[:, 4:5]
    )
    more = jnp.where(spilled > 0, 1, 0).astype(I32)
    fetched(packed, mine, tiles, sems)
    fetched(other, theirs, other_tiles, other_sems)
    extra_at = pl.multiple_of(tiles * TILE, TILE)
    extra_rows = pl.ds(extra_at, SPILL)

    @pl.when(more > 0)
    def _():
        mine[extra_rows, :] = near[...]
        rest = pl.ds(pl.multiple_of(extra_at + SPILL, SPILL), TILE - SPILL)
        mine[rest, :] = jnp.zeros((TILE - SPILL, mine.shape[1]), BF16)
        at = pl.multiple_of(other_tiles * TILE, TILE)
        theirs[pl.ds(at, SPILL), :] = near[...]
        theirs[pl.ds(pl.multiple_of(at + SPILL, SPILL), SPILL), :] = cross[...]
        best[:, pl.ds(extra_at, TILE)] = jnp.full((1, TILE), -1.0, F32)
        score(mine, tiles, tiles + 1, mine, tiles, best, marks)

    score(mine, 0, tiles + more, theirs, other_tiles + more, best, marks)
    flag = jnp.maximum(info[17], other_info[17]).astype(F32)
    reach = 384
    row = iota((16, reach), 0)
    sub, lane = iota((8, EXTRA), 0), iota((8, EXTRA), 1)
    lower = (lane >= sub * BLOCK) & (lane < sub * BLOCK + BLOCK)
    upper = (lane + EXTRA >= sub * BLOCK) & (lane + EXTRA < sub * BLOCK + BLOCK)
    empty = jnp.where(((lane - sub * BLOCK) & (EXTRA - 1)) >= 64, flag, 0.0)
    for step in range(CHIPS // 8):
        first = pl.multiple_of((info[step] >> 7) << 7, 128)
        parts = thirds(best[:, pl.ds(first, reach)])
        stack = jnp.zeros((16, reach), F32)
        for at, part in enumerate(parts):
            stack = jnp.where(row == at, part.astype(F32), stack)
        pick = hot(iota((reach, 2 * EXTRA), 0) + first == spots[step : step + 1, :])
        value = jnp.sum(dot(stack.astype(BF16), pick), 0, keepdims=True)
        line = jnp.where(upper, value[:, EXTRA:], jnp.where(lower, value[:, :EXTRA], empty))
        back[8 * step : 8 * step + 8, :] = line

    @pl.when(more > 0)
    def _():
        fields = fields_of(near[:, width:]).astype(I32)
        filled = fields[4:5, :] > 0
        source = iota((CHIPS, SPILL), 0) == fields[7:8, :]
        line = hot(iota((EXTRA, SPILL), 0) == fields[6:7, :])
        total = back[...]
        for part in thirds(best[:, extra_rows]):
            held = jnp.where(source & filled, part.astype(F32), 0.0).astype(BF16)
            total = total + dot(held, line, COLS)
        back[...] = total


def home_kernel(me, back, place, highest, flag):
    rows = place.shape[1]
    base = (me[0] & 7) * BLOCK
    pick = hot(iota((CHIPS, rows), 0) == place[0:1, :])
    lines = back[...]
    total = jnp.zeros((EXTRA, rows), F32)
    for part in thirds(lines):
        total = total + dot(part, pick, (((0,), (0,)), ((), ())))
    mine = iota((EXTRA, rows), 0) == ((place[1:2, :] + base) & (EXTRA - 1))
    highest[...] = jnp.sum(jnp.where(mine, total, 0.0), 0, keepdims=True)
    marks = ((iota(lines.shape, 1) - base) & (EXTRA - 1)) >= 64
    flag[0] = jnp.max(jnp.where(marks, lines, 0.0)).astype(I32)


def whole(shape):
    return pl.BlockSpec(shape, lambda *_: (0,) * len(shape))


SCALARS = pl.BlockSpec(memory_space=pltpu.SMEM)
PLACED = pl.BlockSpec(memory_space=pl.ANY)
PARAMS = pltpu.CompilerParams(vmem_limit_bytes=56 * 1024 * 1024)


def array(shape, dtype):
    return jax.ShapeDtypeStruct(shape, dtype)


def exchange(x):
    return lax.all_to_all(
        x, BOTH, split_axis=0, concat_axis=0, tiled=True, axis_index_groups=GROUPS
    )


def direct(embed, owner, local_id, rank):
    rows, width = embed.shape
    full = width + EXTRA
    lines = CHIPS * BLOCK
    chunks = lines // CHUNK
    me = ((lax.axis_index("grp") >> 1) * 8 + lax.axis_index("blk")).astype(I32).reshape(1)
    sent, place = pl.pallas_call(
        send_kernel,
        grid=(chunks,),
        in_specs=[SCALARS, whole((rows, width))] + [whole((1, rows))] * 3,
        out_specs=[pl.BlockSpec((CHUNK, width), lambda i: (i, 0)), whole((8, rows))],
        out_shape=[array((lines, width), BF16), array((8, rows), I32)],
        scratch_shapes=[
            pltpu.VMEM((rows, width), BF16),
            pltpu.VMEM((1, rows), I32),
            pltpu.VMEM((CHIPS, width), F32),
        ],
        compiler_params=PARAMS,
        name="send",
    )(me, embed, owner.reshape(1, rows), local_id.reshape(1, rows), rank.reshape(1, rows))
    taken = exchange(sent.reshape(CHIPS, BLOCK, width)).reshape(lines, width)
    spill, spots, fields, info = pl.pallas_call(
        read_kernel,
        in_specs=[PLACED],
        out_specs=[
            whole((SPILL, full)),
            whole((chunks, 2 * EXTRA)),
            whole((chunks, EXTRA, CHUNK)),
            SCALARS,
        ],
        out_shape=[
            array((SPILL, full), BF16),
            array((chunks, 2 * EXTRA), I32),
            array((chunks, EXTRA, CHUNK), BF16),
            array((32,), I32),
        ],
        scratch_shapes=[
            pltpu.VMEM((lines, width), BF16),
            pltpu.VMEM((SPILL, full), F32),
            pltpu.VMEM((chunks, CHUNK), I32),
            pltpu.SemaphoreType.DMA((chunks,)),
        ],
        compiler_params=PARAMS,
        name="read",
    )(taken)
    near = lax.ppermute(spill, BOTH, [(i, i ^ 1) for i in range(2 * CHIPS)])
    packed = pl.pallas_call(
        pack_kernel,
        in_specs=[SCALARS, PLACED, whole((chunks, 2 * EXTRA)), whole((chunks, EXTRA, CHUNK))],
        out_specs=PLACED,
        out_shape=array((PACKED, full), BF16),
        scratch_shapes=[
            pltpu.VMEM((lines, width), BF16),
            pltpu.VMEM((ROOM, full), BF16),
            pltpu.SemaphoreType.DMA((chunks,)),
            pltpu.SemaphoreType.DMA((TILES,)),
        ],
        compiler_params=PARAMS,
        cost_estimate=pl.CostEstimate(
            flops=2 * lines * WINDOW * full, bytes_accessed=4 * lines * full, transcendentals=0
        ),
        name="pack",
    )(info, taken, spots, fields)
    swap = [(i, i ^ 1) for i in range(16)]
    other_info = lax.ppermute(info, "grp", swap)
    other = lax.ppermute(packed, "grp", swap)
    cross = lax.ppermute(near, "grp", swap)
    best = pl.pallas_call(
        own_kernel,
        in_specs=[SCALARS, PLACED],
        out_specs=whole((1, PACKED)),
        out_shape=array((1, PACKED), F32),
        scratch_shapes=[
            pltpu.VMEM((PACKED, full), BF16),
            pltpu.VMEM((PACKED, TILE), I32),
            pltpu.SemaphoreType.DMA((TILES,)),
        ],
        compiler_params=PARAMS,
        cost_estimate=pl.CostEstimate(
            flops=2 * 1024 * 1024 * width, bytes_accessed=2 * PACKED * full, transcendentals=0
        ),
        name="own",
    )(info, packed)
    back = pl.pallas_call(
        other_kernel,
        in_specs=[SCALARS, SCALARS, PLACED, PLACED]
        + [whole((SPILL, full))] * 2
        + [whole((1, PACKED)), whole((chunks, 2 * EXTRA))],
        out_specs=whole((CHIPS, EXTRA)),
        out_shape=array((CHIPS, EXTRA), F32),
        scratch_shapes=[
            pltpu.VMEM((PACKED + TILE, full), BF16),
            pltpu.VMEM((PACKED + TILE, full), BF16),
            pltpu.VMEM((1, PACKED + 2 * TILE), F32),
            pltpu.VMEM((PACKED + TILE, TILE), I32),
            pltpu.SemaphoreType.DMA((TILES,)),
            pltpu.SemaphoreType.DMA((TILES,)),
        ],
        compiler_params=PARAMS,
        name="other",
    )(info, other_info, packed, other, near, cross, best, spots)
    home = exchange(back)
    highest, flag = pl.pallas_call(
        home_kernel,
        in_specs=[SCALARS, whole((CHIPS, EXTRA)), whole((8, rows))],
        out_specs=[whole((1, rows)), SCALARS],
        out_shape=[array((1, rows), F32), array((1,), I32)],
        compiler_params=PARAMS,
        name="home",
    )(me, home, place)
    return highest.reshape(rows), flag[0]


def group_kernel(queries, keys, best_in, best, marks):
    best[...] = best_in[...]
    tiles = keys.shape[0] // TILE
    score(queries, 0, tiles, keys, tiles, best, marks)


def by_group(embed, owner, local_id, rank):
    n_group, n_block = lax.axis_size("grp"), lax.axis_size("blk")
    row_count, columns = embed.shape
    capacity = row_count // 8
    width = n_group * capacity
    full = columns + EXTRA
    wide = embed.astype(F32)
    unit = (wide * lax.rsqrt(jnp.sum(wide * wide, 1, keepdims=True) + EPS)).astype(BF16)
    target = owner[:, 0]
    onehot = (target[:, None] == jnp.arange(n_group, dtype=I32)[None, :]).astype(I32)
    position = jnp.sum((jnp.cumsum(onehot, 0) - 1) * onehot, 1)
    slot_index = target * capacity + position
    fields = jnp.stack([local_id, target, rank >> 8, rank & 255, jnp.ones_like(rank)], 1)
    fields = jnp.pad(fields, ((0, 0), (0, EXTRA - 5))).astype(BF16)
    sent = jnp.zeros((width, full), BF16).at[slot_index].set(jnp.concatenate([unit, fields], 1))
    routed = lax.all_to_all(
        sent.reshape(n_group, capacity, full), "grp", split_axis=0, concat_axis=0, tiled=True
    ).reshape(width, full)
    best = jnp.full((1, width), -1.0, F32)
    for by in range(n_block):
        turn = [(i, (i + by) % n_block) for i in range(n_block)]
        best = pl.pallas_call(
            group_kernel,
            in_specs=[whole((width, full))] * 2 + [whole((1, width))],
            out_specs=whole((1, width)),
            out_shape=array((1, width), F32),
            scratch_shapes=[pltpu.VMEM((width, TILE), I32)],
            compiler_params=PARAMS,
            name="group",
        )(routed, lax.ppermute(routed, "blk", turn) if by else routed, best)
    home = lax.all_to_all(
        best.reshape(n_group, capacity), "grp", split_axis=0, concat_axis=0, tiled=True
    )
    return home.reshape(width)[slot_index]


def per_device(embed, owner, local_id, rank):
    highest, flag = direct(embed, owner, local_id, rank)
    return lax.cond(
        flag > 0, lambda: by_group(embed, owner, local_id, rank), lambda: highest
    )


def solution(mesh):
    in_specs = (
        P(("grp", "blk"), None),
        P(("grp", "blk"), None),
        P(("grp", "blk")),
        P(("grp", "blk")),
    )
    out_specs = P(("grp", "blk"))
    return jax.shard_map(
        per_device, mesh=mesh, in_specs=in_specs, out_specs=out_specs, check_vma=False
    )
```

time: 953 us -> 127 us (0.13); the launches traced: 943 us -> 127 us
  loops' own time: 407 us -> 0.31 us
  local copies, waits for them, and re-layouts: 196 us -> 3.7 us
  waiting for transfers between devices: 128 us -> 18.5 us
  starting transfers between devices: 91.1 us -> 18.1 us
  matrix products: 32.4 us -> 0 us
  Pallas kernels: 0 us -> 32.1 us
  other arithmetic: 18.2 us -> 0 us
  between operations: 13.6 us -> 0.9 us
    another operation x133 -> x1, loops' own time: 407 us -> 0.31 us  [per_device(): lax.cond(flag > 0, lambda: by_group(embed, owner, local_id, rank), lambda...]
    dynamic_slice x291 -> x0, local copies, waits for them, and re-layouts: 161 us -> none  [the longest x279 156 us: outer(): row_best, columns = lax.scan(inner, empty, key_tiles)]
    all_gather x1 -> x0, waiting for transfers between devices: 95.4 us -> none  [per_device(): keys = lax.all_gather(query, 'blk', axis=0, tiled=True)]
    all_to_all x4 -> x1, starting transfers between devices: 91.1 us -> 17 us  [exchange(): lax.all_to_all(x, BOTH, split_axis=0, concat_axis=0, tiled=True, axis_ind...]
    all_gather x2 -> x0, blocking collectives: 56.5 us -> none  [the longest x1 28.3 us: per_device(): key_rank = lax.all_gather(query_rank, 'blk', axis=0, tiled=True)]
    all_to_all x0 -> x1, blocking collectives: none -> 53 us  [exchange(): lax.all_to_all(x, BOTH, split_axis=0, concat_axis=0, tiled=True, axis_ind...]
    dot_general x23 -> x0, matrix products: 32.4 us -> none  [pair_scores(): lax.dot_general(query, keys, (((1,), (1,)), ((), ())), preferred_element_...]
    pallas_call x0 -> x6, Pallas kernels: none -> 32.1 us  [the longest x1 6.89 us: direct(): pl.pallas_call(other_kernel, in_specs=[SCALARS, SCALARS, PLACED, PLACED]...]
  transfers between devices with their start and end apart: 5 -> 5, of which waited for: 4 -> 2; matrix products, arithmetic and copies ran while one was open for 3% -> 0% of each run, Pallas kernels for 0% -> 4%
where the time goes in v1:
time: 127 us
  blocking collectives  53 us (42%)
  Pallas kernels  32.1 us (25%)
  waiting for transfers between devices  18.5 us (15%)
  starting transfers between devices  18.1 us (14%)
  local copies, waits for them, and re-layouts  3.7 us (3%)
    all_to_all x1, blocking collectives, exchange(): lax.all_to_all(x, BOTH, split_axis=0, concat_axis=0, tiled=True, axis_ind...  53 us
    all_to_all x1, starting transfers between devices, exchange(): lax.all_to_all(x, BOTH, split_axis=0, concat_axis=0, tiled=True, axis_ind...  17 us
    all_to_all x1, waiting for transfers between devices, exchange(): lax.all_to_all(x, BOTH, split_axis=0, concat_axis=0, tiled=True, axis_ind...  9.55 us
    ppermute x1, waiting for transfers between devices, direct(): near = lax.ppermute(spill, BOTH, [(i, i ^ 1) for i in range(2 * CHIPS)])  8.98 us
    pallas_call x1, Pallas kernels, direct(): pl.pallas_call(other_kernel, in_specs=[SCALARS, SCALARS, PLACED, PLACED]...  6.89 us
    pallas_call x1, Pallas kernels, direct(): pl.pallas_call(send_kernel, grid=(chunks,), in_specs=[SCALARS, whole((row...  6.79 us
    pallas_call x1, Pallas kernels, direct(): pl.pallas_call(pack_kernel, in_specs=[SCALARS, PLACED, whole((chunks, 2 *...  6.07 us
    pallas_call x1, Pallas kernels, direct(): pl.pallas_call(own_kernel, in_specs=[SCALARS, PLACED], out_specs=whole((1...  5.49 us
  transfers between devices with their start and end apart: 5, of which 2 were waited for; matrix products, arithmetic and copies ran while one was open for 0% of the time, Pallas kernels for 4%

profile of v1, /device:TPU:0, one launch (start us, length us, event | category | flops | bytes accessed | tf_op | source)
XLA Modules:
  0.0 126.6 jit_solution(16358859906375173792)
XLA Ops:
  0.0 6.8 %send.1 = (bf16[1536,1024]{1,0:T(8,128)(2,1)}, s32[8,512]{1,0:T(8,128)}) custom-call(s32[1]{0:T(128)} %bitcast.9.me, bf16[512,1024]{1,0:T(8,128)(2,1)} %embed.1, s32[1,512]{1,0:T(1,128)} %bitcast.57, s32[1,512]{1,0:T(1,128)} %bitcast.60, s32[1,512]{1,0:T(1,128)} %bitcast.61), custom_call_target="tpu_custom_call" | custom-call | tf_op jit(solution)/shard_map/send/pallas_call | solution.py:369
  6.8 53.0 %all_to_all.28 = bf16[64,24,1024]{2,1,0:T(8,128)(2,1)} all-to-all(bf16[64,24,1024]{2,1,0:T(8,128)(2,1)} %bitcast.54), channel_id=1, replica_groups={{0,1,2,3,4,5,6,7,16,17,18,19,20,21,22,23,32,33,34,35,36,37,38,39,48,49,..., dimensions={0} | all-to-all | bytes 6291456 | tf_op jit(solution)/shard_map/all_to_all | solution.py:358
  59.8 5.4 %read.1 = (bf16[128,1152]{1,0:T(8,128)(2,1)}, s32[8,256]{1,0:T(8,128)}, bf16[8,128,192]{2,1,0:T(8,128)(2,1)}, s32[32]{0:T(128)}) custom-call(bf16[1536,1024]{1,0:T(8,128)(2,1)} %bitcast.51), custom_call_target="tpu_custom_call" | custom-call | tf_op jit(solution)/shard_map/read/pallas_call | solution.py:384
  65.2 0.0 copy-start.15
  65.2 0.0 copy-start.13
  65.2 6.1 %pack.1.packed = bf16[1536,1152]{1,0:T(8,128)(2,1)} custom-call(s32[32]{0:T(128)} %get-tuple-element.32.info, bf16[1536,1024]{1,0:T(8,128)(2,1)} %bitcast.52, s32[8,256]{1,0:T(8,128)} %get-tuple-element.33.spots, bf16[8,128,192]{2,1,0:T(8,128)(2,1)} %get-tuple-element.34.fields), custom_call_target="tpu_custom_call" | custom-call | flops 736100352 | bytes 7077888 | tf_op jit(solution)/shard_map/pack/pallas_call | solution.py:409
  71.3 0.1 collective-permute-start.8
  71.3 0.0 copy-done.15
  71.4 0.4 collective-permute-start.9
  71.8 9.0 %collective-permute-done.9.near = bf16[128,1152]{1,0:T(8,128)(2,1)S(1)} collective-permute-done((bf16[128,1152]{1,0:T(8,128)(2,1)S(1)}, bf16[128,1152]{1,0:T(8,128)(2,1)S(1)}, u32[]{:S(2)}, u32[]{:S(2)}) %collective-permute-start.9) | collective-permute-done | bytes 294944 | tf_op jit(solution)/shard_map/ppermute | solution.py:408
  80.8 0.0 copy-start.7
  80.8 0.0 collective-permute-start.10
  80.8 0.0 copy-done.13
  80.8 0.5 collective-permute-start.7
  81.3 5.5 %own.1.best_in = f32[1,1536]{1,0:T(1,128)} custom-call(s32[32]{0:T(128)} %get-tuple-element.32.info, bf16[1536,1152]{1,0:T(8,128)(2,1)} %pack.1.packed), custom_call_target="tpu_custom_call" | custom-call | flops 2147483648 | bytes 3538944 | tf_op jit(solution)/shard_map/own/pallas_call | solution.py:430
  86.8 0.0 copy-done.7
  86.8 0.0 copy-start.1
  86.8 0.0 copy-start.10
  86.8 0.0 copy-start.11
  86.8 0.0 copy-start.12
  86.8 0.0 collective-permute-done.7.other_info
  86.9 0.0 copy-start.14
  86.9 0.0 collective-permute-done.10.cross
  86.9 0.0 copy-start.8
  86.9 0.0 collective-permute-done.8.other
  86.9 0.5 copy-done.14
  87.4 0.2 copy-done.8
  87.6 0.0 copy-start.2
  87.6 1.8 %copy-done.2 = bf16[1536,1152]{1,0:T(8,128)(2,1)} copy-done((bf16[1536,1152]{1,0:T(8,128)(2,1)}, bf16[1536,1152]{1,0:T(8,128)(2,1)S(1)}, u32[]{:S(2)}) %copy-start.2) | copy-done | bytes 3538968
  89.4 6.9 %other.1 = f32[64,128]{1,0:T(8,128)} custom-call(s32[32]{0:T(128)} %get-tuple-element.32.info, s32[32]{0:T(128)} %copy-done.14, bf16[1536,1152]{1,0:T(8,128)(2,1)} %pack.1.packed, bf16[1536,1152]{1,0:T(8,128)(2,1)} %copy-done.2, bf16[128,1152]{1,0:T(8,128)(2,1)} %copy-done.7, bf16[128,1152]{1,0:T(8,128)(2,1)} %copy-done.8, f32[1,1536]{1,0:T(1,128)} %own.1.best_in, ...), custom_call_target="tpu_custom_call" | custom-call | tf_op jit(solution)/shard_map/other/pallas_call | solution.py:446
  96.3 17.0 %all-to-all-start.3 = ((f32[64,1,128]{2,1,0:T(1,128)}), f32[64,1,128]{2,1,0:T(1,128)S(1)}, u32[]{:S(2)}, u32[]{:S(2)}) async-start(f32[64,1,128]{2,1,0:T(1,128)} %bitcast.55), calls=%async_computation.3 | async-start | bytes 65536 | tf_op jit(solution)/shard_map/all_to_all | solution.py:358
  113.3 9.6 %all-to-all-done.3 = f32[64,1,128]{2,1,0:T(1,128)S(1)} async-done(((f32[64,1,128]{2,1,0:T(1,128)}), f32[64,1,128]{2,1,0:T(1,128)S(1)}, u32[]{:S(2)}, u32[]{:S(2)}) %all-to-all-start.3) | async-done | bytes 32800 | tf_op jit(solution)/shard_map/all_to_all | solution.py:358
  122.9 0.0 copy-start.9
  122.9 0.6 copy-done.9
  123.5 1.5 %home.1 = (f32[1,512]{1,0:T(1,128)S(1)}, s32[1]{0:T(128)}) custom-call(s32[1]{0:T(128)} %bitcast.9.me, f32[64,128]{1,0:T(8,128)} %bitcast.56, s32[8,512]{1,0:T(8,128)} %get-tuple-element.36.place), custom_call_target="tpu_custom_call" | custom-call | tf_op jit(solution)/shard_map/home/pallas_call | solution.py:465
  125.6 0.0 copy-done.1
  125.6 0.0 copy-done.10
  125.7 0.0 copy-done.11
  125.7 0.0 copy-done.12
  125.7 0.3 conditional.1
  126.0 0.0 copy-start.16
  126.0 0.6 copy-done.16
Async XLA Ops:
  65.2 6.2 %copy-start.15 = (bf16[128,1152]{1,0:T(8,128)(2,1)S(1)}, bf16[128,1152]{1,0:T(8,128)(2,1)}, u32[]{:S(2)}) copy-start(bf16[128,1152]{1,0:T(8,128)(2,1)} %get-tuple-element.35) | copy-start | bytes 884740
  65.2 15.6 %copy-start.13 = (s32[32]{0:T(128)S(1)}, s32[32]{0:T(128)}, u32[]{:S(2)}) copy-start(s32[32]{0:T(128)} %get-tuple-element.32.info) | copy-start | bytes 388
  71.3 15.6 %collective-permute-start.8 = (bf16[1536,1152]{1,0:T(8,128)(2,1)}, bf16[1536,1152]{1,0:T(8,128)(2,1)S(1)}, u32[]{:S(2)}, u32[]{:S(2)}) collective-permute-start(bf16[1536,1152]{1,0:T(8,128)(2,1)} %pack.1.packed), channel_id=1, source_target_pairs={{0,8},{8,0},{16,24},{24,16},{32,40},{40,32},{48,56},{56,48},{64,72... | collective-permute-start | bytes 10616840 | tf_op jit(solution)/shard_map/ppermute | solution.py:428
  71.4 9.4 %collective-permute-start.9 = (bf16[128,1152]{1,0:T(8,128)(2,1)S(1)}, bf16[128,1152]{1,0:T(8,128)(2,1)S(1)}, u32[]{:S(2)}, u32[]{:S(2)}) collective-permute-start(bf16[128,1152]{1,0:T(8,128)(2,1)S(1)} %copy-done.15), channel_id=1, source_target_pairs={{0,1},{1,0},{2,3},{3,2},{4,5},{5,4},{6,7},{7,6},{8,9},{9,8},{10,11... | collective-permute-start | bytes 884744 | tf_op jit(solution)/shard_map/ppermute | solution.py:408
  80.8 6.0 %copy-start.7 = (bf16[128,1152]{1,0:T(8,128)(2,1)}, bf16[128,1152]{1,0:T(8,128)(2,1)S(1)}, u32[]{:S(2)}) copy-start(bf16[128,1152]{1,0:T(8,128)(2,1)S(1)} %collective-permute-done.9.near) | copy-start | bytes 884740
  80.8 6.1 %collective-permute-start.10 = (bf16[128,1152]{1,0:T(8,128)(2,1)S(1)}, bf16[128,1152]{1,0:T(8,128)(2,1)S(1)}, u32[]{:S(2)}, u32[]{:S(2)}) collective-permute-start(bf16[128,1152]{1,0:T(8,128)(2,1)S(1)} %collective-permute-done.9.near), channel_id=1, source_target_pairs={{0,8},{8,0},{16,24},{24,16},{32,40},{40,32},{48,56},{56,48},{64,72... | collective-permute-start | bytes 884744 | tf_op jit(solution)/shard_map/ppermute | solution.py:429
  80.8 6.1 %collective-permute-start.7 = (s32[32]{0:T(128)S(1)}, s32[32]{0:T(128)S(1)}, u32[]{:S(2)}, u32[]{:S(2)}) collective-permute-start(s32[32]{0:T(128)S(1)} %copy-done.13), channel_id=1, source_target_pairs={{0,8},{8,0},{16,24},{24,16},{32,40},{40,32},{48,56},{56,48},{64,72... | collective-permute-start | bytes 392 | tf_op jit(solution)/shard_map/ppermute | solution.py:427
  86.8 38.8 %copy-start.1 = (bf16[512,1024]{1,0:T(8,128)(2,1)S(1)}, bf16[512,1024]{1,0:T(8,128)(2,1)}, u32[]{:S(2)}) copy-start(bf16[512,1024]{1,0:T(8,128)(2,1)} %embed.1) | copy-start | bytes 3145732
  86.8 38.8 %copy-start.10 = (s32[512,1]{0,1:T(1,128)S(1)}, s32[512,1]{0,1:T(1,128)}, u32[]{:S(2)}) copy-start(s32[512,1]{0,1:T(1,128)} %param.7) | copy-start | bytes 6148
  86.8 38.8 %copy-start.11 = (s32[512]{0:T(512)S(1)}, s32[512]{0:T(512)}, u32[]{:S(2)}) copy-start(s32[512]{0:T(512)} %param.8) | copy-start | bytes 6148
  86.8 38.8 %copy-start.12 = (s32[512]{0:T(512)S(1)}, s32[512]{0:T(512)}, u32[]{:S(2)}) copy-start(s32[512]{0:T(512)} %param.9) | copy-start | bytes 6148
  86.9 0.6 copy-start.14
  86.9 0.7 copy-start.8
  87.6 1.8 %copy-start.2 = (bf16[1536,1152]{1,0:T(8,128)(2,1)}, bf16[1536,1152]{1,0:T(8,128)(2,1)S(1)}, u32[]{:S(2)}) copy-start(bf16[1536,1152]{1,0:T(8,128)(2,1)S(1)} %collective-permute-done.8.other) | copy-start | bytes 10616836
  96.3 26.6 %all-to-all-start.3 = ((f32[64,1,128]{2,1,0:T(1,128)}), f32[64,1,128]{2,1,0:T(1,128)S(1)}, u32[]{:S(2)}, u32[]{:S(2)}) async-start(f32[64,1,128]{2,1,0:T(1,128)} %bitcast.55), calls=%async_computation.3 | async-start | bytes 65536 | tf_op jit(solution)/shard_map/all_to_all | solution.py:358
  122.9 0.6 copy-start.9
  126.0 0.6 copy-start.16

commit v2 on v1

--- a/solution.py
+++ b/solution.py
@@ -123,12 +123,11 @@
     return copies
 
 
-def read_kernel(source, spill, spots, fields, info, taken, pile, strange, copied):
+def read_kernel(source, spill, spots, fields, info, taken, pile, ends, strange, copied):
     chunks = taken.shape[0] // CHUNK
     width = taken.shape[1]
     copies = load_chunks(source, taken, copied)
     upto = hot(iota((CHUNK, CHUNK), 0) <= iota((CHUNK, CHUNK), 1))
-    ends = hot(iota((16, CHUNK), 1) == iota((16, CHUNK), 0) * BLOCK + SEATS)
     place = iota((EXTRA, CHUNK), 1)
     sender = jnp.zeros(place.shape, I32)
     for at in range(1, 8):
@@ -136,33 +135,45 @@
     spread = hot(place - sender * BLOCK == iota((EXTRA, CHUNK), 0))
     mine = (iota((64, CHUNK), 0) & 7) == sender[:64, :]
     spots[...] = jnp.full(spots.shape, -1, I32)
-    start, start_strange = jnp.int32(0), jnp.int32(0)
-    late = jnp.zeros((8, 1), F32)
+    for copy in copies:
+        copy.wait()
+    for at in range(CHIPS):
+        last = at * BLOCK + SEATS
+        top = (last // 16) * 16
+        tile = taken[top : top + 16, :].astype(F32)
+        ends[at : at + 1, :] = tile[last - top : last - top + 1, :]
+    late = jnp.max(ends[:, EXTRA - 1 : EXTRA])
+    stack = [
+        ends[8 * at : 8 * at + 8, EXTRA * f : EXTRA * (f + 1)]
+        for at in range(chunks)
+        for f in range(8)
+    ]
+    wide = dot(jnp.concatenate(stack, 0).astype(BF16), spread)
+    natives, foreigns = [], []
     for at in range(chunks):
-        copies[at].wait()
-        rows = pl.ds(at * CHUNK, CHUNK)
-        lines = dot(ends, taken[rows, :])[:8, :]
-        late = jnp.maximum(late, lines[:, EXTRA - 1 : EXTRA])
-        stack = [lines[:, EXTRA * f : EXTRA * (f + 1)] for f in range(8)]
-        wide = dot(jnp.concatenate(stack, 0).astype(BF16), spread)
-        wide = jnp.where(mine, wide, 0.0)
-        found = [jnp.sum(wide[8 * f : 8 * f + 8, :], 0, keepdims=True) for f in range(8)]
+        part = jnp.where(mine, wide[64 * at : 64 * at + 64, :], 0.0)
+        found = [jnp.sum(part[8 * f : 8 * f + 8, :], 0, keepdims=True) for f in range(8)]
         table = jnp.concatenate(found + [jnp.zeros((EXTRA - 8, CHUNK), F32)], 0)
         fields[at] = table.astype(BF16)
-        foreign = found[5]
-        native = found[4] - foreign
-        both = jnp.where(iota((16, CHUNK), 0) == 0, native, foreign)
-        running = dot(both.astype(BF16), upto).astype(I32)
-        spots[at : at + 1, 0:CHUNK] = jnp.where(native > 0, running[0:1, :] + (start - 1), -1)
+        natives.append(found[4] - found[5])
+        foreigns.append(found[5])
+    both = jnp.concatenate(natives + foreigns, 0)
+    running = dot(both.astype(BF16), upto).astype(I32)
+    start, start_strange = jnp.int32(0), jnp.int32(0)
+    for at in range(chunks):
+        native, foreign = natives[at], foreigns[at]
+        spots[at : at + 1, 0:CHUNK] = jnp.where(
+            native > 0, running[at : at + 1, :] + (start - 1), -1
+        )
         strange[at : at + 1, :] = jnp.where(
-            foreign > 0, running[1:2, :] + (start_strange - 1), -1
+            foreign > 0, running[chunks + at : chunks + at + 1, :] + (start_strange - 1), -1
         )
         info[at] = (start >> 4) << 4
         start = start + jnp.sum(native).astype(I32)
         start_strange = start_strange + jnp.sum(foreign).astype(I32)
-    full = (start > PACKED) | (start_strange > SPILL) | (jnp.max(late) > 0)
-    info[16] = jnp.minimum((start + TILE - 1) // TILE, TILES)
-    info[17] = jnp.where(full, 1, 0)
+    info[16] = (start + TILE - 1) // TILE
+    info[17] = jnp.where((start_strange > SPILL) | (late > 0), 1, 0)
+    info[18] = start
     pile[...] = jnp.zeros(pile.shape, F32)
 
     @pl.when(start_strange > 0)
@@ -209,6 +220,55 @@
             pl.when(at < tiles)(copy.wait if wait else copy.start)
 
 
+def append_kernel(info, near, packed_in, packed, info_out, window, blank, sems):
+    for at in range(20):
+        info_out[at] = info[at]
+    total, tiles = info[18], info[16]
+    count = jnp.sum(near[:, packed.shape[1] - EXTRA :].astype(F32)[:, 4:5]).astype(I32)
+    first = (total >> 4) << 4
+    fits = (total + count <= PACKED) & (first + SPILL + 16 <= PACKED)
+
+    @pl.when((count > 0) & jnp.logical_not(fits))
+    def _():
+        info_out[17] = 1
+
+    @pl.when((count > 0) & fits)
+    def _():
+        more = (total + count + TILE - 1) // TILE
+        info_out[16] = more
+        begin = pl.multiple_of(first, 16)
+        head = pltpu.make_async_copy(
+            packed.at[pl.ds(begin, 16), :], window.at[pl.ds(0, 16), :], sems.at[0]
+        )
+        head.start()
+
+        @pl.when(more > tiles)
+        def _():
+            blank[...] = jnp.zeros(blank.shape, BF16)
+
+        shift = iota((SPILL + 16, SPILL), 0) - iota((SPILL + 16, SPILL), 1)
+        moved = dot(hot(shift == total - first), near[...])
+        head.wait()
+        keep = iota((16, packed.shape[1]), 0) < total - first
+        window[0:16, :] = jnp.where(
+            keep, window[0:16, :].astype(F32), moved[:16]
+        ).astype(BF16)
+        window[16:, :] = moved[16:].astype(BF16)
+
+        @pl.when(more > tiles)
+        def _():
+            at = pl.multiple_of(tiles * TILE, TILE)
+            clear = pltpu.make_async_copy(blank, packed.at[pl.ds(at, TILE), :], sems.at[1])
+            clear.start()
+            clear.wait()
+
+        put = pltpu.make_async_copy(
+            window, packed.at[pl.ds(begin, SPILL + 16), :], sems.at[2]
+        )
+        put.start()
+        put.wait()
+
+
 def score(queries, low, high, keys, key_tiles, best, marks):
     width = queries.shape[1] - EXTRA
 
@@ -266,63 +326,53 @@
 
 
 def other_kernel(
-    info, other_info, packed, other, near, cross, best_in, spots, back,
+    info, other_info, packed, other, near, best_in, spots, back,
     mine, theirs, best, marks, sems, other_sems,
 ):
     tiles, other_tiles = info[16], other_info[16]
-    width = mine.shape[1] - EXTRA
     fetch(packed, mine, tiles, sems)
     fetch(other, theirs, other_tiles, other_sems)
     best[:, :PACKED] = best_in[...]
     best[:, PACKED:] = jnp.full((1, best.shape[1] - PACKED), -1.0, F32)
-    spilled = jnp.max(near[:, width:].astype(F32)[:, 4:5]) + jnp.max(
-        cross[:, width:].astype(F32)[:, 4:5]
-    )
-    more = jnp.where(spilled > 0, 1, 0).astype(I32)
     fetched(packed, mine, tiles, sems)
     fetched(other, theirs, other_tiles, other_sems)
-    extra_at = pl.multiple_of(tiles * TILE, TILE)
-    extra_rows = pl.ds(extra_at, SPILL)
-
-    @pl.when(more > 0)
-    def _():
-        mine[extra_rows, :] = near[...]
-        rest = pl.ds(pl.multiple_of(extra_at + SPILL, SPILL), TILE - SPILL)
-        mine[rest, :] = jnp.zeros((TILE - SPILL, mine.shape[1]), BF16)
-        at = pl.multiple_of(other_tiles * TILE, TILE)
-        theirs[pl.ds(at, SPILL), :] = near[...]
-        theirs[pl.ds(pl.multiple_of(at + SPILL, SPILL), SPILL), :] = cross[...]
-        best[:, pl.ds(extra_at, TILE)] = jnp.full((1, TILE), -1.0, F32)
-        score(mine, tiles, tiles + 1, mine, tiles, best, marks)
-
-    score(mine, 0, tiles + more, theirs, other_tiles + more, best, marks)
+    score(mine, 0, tiles, theirs, other_tiles, best, marks)
     flag = jnp.maximum(info[17], other_info[17]).astype(F32)
     reach = 384
     row = iota((16, reach), 0)
+
+    def stacked(first, count):
+        parts = thirds(best[:, pl.ds(pl.multiple_of(first, 128), count)])
+        stack = jnp.zeros((16, count), F32)
+        for at, part in enumerate(parts):
+            stack = jnp.where(row[:, :count] == at, part.astype(F32), stack)
+        return stack.astype(BF16)
+
     sub, lane = iota((8, EXTRA), 0), iota((8, EXTRA), 1)
     lower = (lane >= sub * BLOCK) & (lane < sub * BLOCK + BLOCK)
     upper = (lane + EXTRA >= sub * BLOCK) & (lane + EXTRA < sub * BLOCK + BLOCK)
     empty = jnp.where(((lane - sub * BLOCK) & (EXTRA - 1)) >= 64, flag, 0.0)
     for step in range(CHIPS // 8):
-        first = pl.multiple_of((info[step] >> 7) << 7, 128)
-        parts = thirds(best[:, pl.ds(first, reach)])
-        stack = jnp.zeros((16, reach), F32)
-        for at, part in enumerate(parts):
-            stack = jnp.where(row == at, part.astype(F32), stack)
+        first = (info[step] >> 7) << 7
         pick = hot(iota((reach, 2 * EXTRA), 0) + first == spots[step : step + 1, :])
-        value = jnp.sum(dot(stack.astype(BF16), pick), 0, keepdims=True)
+        value = jnp.sum(dot(stacked(first, reach), pick), 0, keepdims=True)
         line = jnp.where(upper, value[:, EXTRA:], jnp.where(lower, value[:, :EXTRA], empty))
         back[8 * step : 8 * step + 8, :] = line
-
-    @pl.when(more > 0)
+    fields = fields_of(near[:, mine.shape[1] - EXTRA :]).astype(I32)
+    filled = fields[4:5, :] > 0
+
+    @pl.when(jnp.max(fields[4:5, :].astype(F32)) > 0)
     def _():
-        fields = fields_of(near[:, width:]).astype(I32)
-        filled = fields[4:5, :] > 0
-        source = iota((CHIPS, SPILL), 0) == fields[7:8, :]
+        total = info[18]
+        first = (total >> 7) << 7
+        shift = iota((2 * EXTRA, SPILL), 0) - iota((2 * EXTRA, SPILL), 1)
+        pick = hot(shift == total - first)
+        value = jnp.sum(dot(stacked(first, 2 * EXTRA), pick), 0, keepdims=True)
+        source = (iota((CHIPS, SPILL), 0) == fields[7:8, :]) & filled
         line = hot(iota((EXTRA, SPILL), 0) == fields[6:7, :])
         total = back[...]
-        for part in thirds(best[:, extra_rows]):
-            held = jnp.where(source & filled, part.astype(F32), 0.0).astype(BF16)
+        for part in thirds(value):
+            held = jnp.where(source, part.astype(F32), 0.0).astype(BF16)
             total = total + dot(held, line, COLS)
         back[...] = total
 
@@ -347,7 +397,7 @@
 
 SCALARS = pl.BlockSpec(memory_space=pltpu.SMEM)
 PLACED = pl.BlockSpec(memory_space=pl.ANY)
-PARAMS = pltpu.CompilerParams(vmem_limit_bytes=56 * 1024 * 1024)
+PARAMS = pltpu.CompilerParams(vmem_limit_bytes=63 * 1024 * 1024)
 
 
 def array(shape, dtype):
@@ -399,6 +449,7 @@
         scratch_shapes=[
             pltpu.VMEM((lines, width), BF16),
             pltpu.VMEM((SPILL, full), F32),
+            pltpu.VMEM((CHIPS, width), F32),
             pltpu.VMEM((chunks, CHUNK), I32),
             pltpu.SemaphoreType.DMA((chunks,)),
         ],
@@ -423,10 +474,23 @@
         ),
         name="pack",
     )(info, taken, spots, fields)
+    packed, info = pl.pallas_call(
+        append_kernel,
+        in_specs=[SCALARS, whole((SPILL, full)), PLACED],
+        out_specs=[PLACED, SCALARS],
+        out_shape=[array((PACKED, full), BF16), array((32,), I32)],
+        scratch_shapes=[
+            pltpu.VMEM((SPILL + 16, full), BF16),
+            pltpu.VMEM((TILE, full), BF16),
+            pltpu.SemaphoreType.DMA((3,)),
+        ],
+        input_output_aliases={2: 0},
+        compiler_params=PARAMS,
+        name="append",
+    )(info, near, packed)
     swap = [(i, i ^ 1) for i in range(16)]
     other_info = lax.ppermute(info, "grp", swap)
     other = lax.ppermute(packed, "grp", swap)
-    cross = lax.ppermute(near, "grp", swap)
     best = pl.pallas_call(
         own_kernel,
         in_specs=[SCALARS, PLACED],
@@ -446,21 +510,20 @@
     back = pl.pallas_call(
         other_kernel,
         in_specs=[SCALARS, SCALARS, PLACED, PLACED]
-        + [whole((SPILL, full))] * 2
-        + [whole((1, PACKED)), whole((chunks, 2 * EXTRA))],
+        + [whole((SPILL, full)), whole((1, PACKED)), whole((chunks, 2 * EXTRA))],
         out_specs=whole((CHIPS, EXTRA)),
         out_shape=array((CHIPS, EXTRA), F32),
         scratch_shapes=[
-            pltpu.VMEM((PACKED + TILE, full), BF16),
-            pltpu.VMEM((PACKED + TILE, full), BF16),
+            pltpu.VMEM((PACKED, full), BF16),
+            pltpu.VMEM((PACKED, full), BF16),
             pltpu.VMEM((1, PACKED + 2 * TILE), F32),
-            pltpu.VMEM((PACKED + TILE, TILE), I32),
+            pltpu.VMEM((PACKED, TILE), I32),
             pltpu.SemaphoreType.DMA((TILES,)),
             pltpu.SemaphoreType.DMA((TILES,)),
         ],
         compiler_params=PARAMS,
         name="other",
-    )(info, other_info, packed, other, near, cross, best, spots)
+    )(info, other_info, packed, other, near, best, spots)
     home = exchange(back)
     highest, flag = pl.pallas_call(
         home_kernel,

time: 127 us -> 117 us (0.921)
  waiting for transfers between devices: 18.5 us -> 12.5 us
  Pallas kernels: 32.1 us -> 29 us
  local copies, waits for them, and re-layouts: 3.7 us -> 1.99 us
    ppermute x1, waiting for transfers between devices: 8.98 us -> 1.06 us  [direct(): near = lax.ppermute(spill, BOTH, [(i, i ^ 1) for i in range(2 * CHIPS)])]
    pallas_call x1, Pallas kernels: 5.4 us -> 3.43 us  [direct(): pl.pallas_call(read_kernel, in_specs=[PLACED], out_specs=[whole((SPILL, f...]
    pallas_call x0 -> x1, Pallas kernels: none -> 1.72 us  [direct(): pl.pallas_call(append_kernel, in_specs=[SCALARS, whole((SPILL, full)), PL...]
    unnamed x24 -> x14, local copies, waits for them, and re-layouts: 3.7 us -> 1.99 us
    pallas_call x1, Pallas kernels: 5.49 us -> 4.13 us  [direct(): pl.pallas_call(own_kernel, in_specs=[SCALARS, PLACED], out_specs=whole((1...]
    ppermute x1, waiting for transfers between devices: 0.01 us -> 1.36 us  [direct(): other_info = lax.ppermute(info, 'grp', swap)]
    pallas_call x1, Pallas kernels: 6.89 us -> 5.57 us  [direct(): pl.pallas_call(other_kernel, in_specs=[SCALARS, SCALARS, PLACED, PLACED]...]
  transfers between devices with their start and end apart: 5 -> 4, of which waited for: 2 -> 4; matrix products, arithmetic and copies ran while one was open for 0% -> 0% of each run, Pallas kernels for 4% -> 9%
where the time goes in v2:
time: 117 us; the launch traced here: 115 us
  blocking collectives  53 us (45%)
  Pallas kernels  29 us (25%)
  starting transfers between devices  17.9 us (15%)
  waiting for transfers between devices  12.5 us (11%)
  local copies, waits for them, and re-layouts  1.99 us (2%)
    all_to_all x1, blocking collectives, exchange(): lax.all_to_all(x, BOTH, split_axis=0, concat_axis=0, tiled=True, axis_ind...  53 us
    all_to_all x1, starting transfers between devices, exchange(): lax.all_to_all(x, BOTH, split_axis=0, concat_axis=0, tiled=True, axis_ind...  16.7 us
    all_to_all x1, waiting for transfers between devices, exchange(): lax.all_to_all(x, BOTH, split_axis=0, concat_axis=0, tiled=True, axis_ind...  9.56 us
    pallas_call x1, Pallas kernels, direct(): pl.pallas_call(send_kernel, grid=(chunks,), in_specs=[SCALARS, whole((row...  6.81 us
    pallas_call x1, Pallas kernels, direct(): pl.pallas_call(pack_kernel, in_specs=[SCALARS, PLACED, whole((chunks, 2 *...  5.81 us
    pallas_call x1, Pallas kernels, direct(): pl.pallas_call(other_kernel, in_specs=[SCALARS, SCALARS, PLACED, PLACED]...  5.57 us
    pallas_call x1, Pallas kernels, direct(): pl.pallas_call(own_kernel, in_specs=[SCALARS, PLACED], out_specs=whole((1...  4.13 us
    pallas_call x1, Pallas kernels, direct(): pl.pallas_call(read_kernel, in_specs=[PLACED], out_specs=[whole((SPILL, f...  3.43 us
  transfers between devices with their start and end apart: 4, of which 4 were waited for; matrix products, arithmetic and copies ran while one was open for 0% of the time, Pallas kernels for 9%

profile of v2, /device:TPU:0, one launch (start us, length us, event | category | flops | bytes accessed | tf_op | source)
XLA Modules:
  0.0 115.4 jit_solution(11581854495723240910)
XLA Ops:
  0.0 6.8 %send.1 = (bf16[1536,1024]{1,0:T(8,128)(2,1)}, s32[8,512]{1,0:T(8,128)}) custom-call(s32[1]{0:T(128)} %bitcast.9.me, bf16[512,1024]{1,0:T(8,128)(2,1)} %embed.1, s32[1,512]{1,0:T(1,128)} %bitcast.41, s32[1,512]{1,0:T(1,128)} %bitcast.44, s32[1,512]{1,0:T(1,128)} %bitcast.45), custom_call_target="tpu_custom_call" | custom-call | tf_op jit(solution)/shard_map/send/pallas_call | solution.py:419
  6.8 53.0 %all_to_all.28 = bf16[64,24,1024]{2,1,0:T(8,128)(2,1)} all-to-all(bf16[64,24,1024]{2,1,0:T(8,128)(2,1)} %bitcast.38), channel_id=1, replica_groups={{0,1,2,3,4,5,6,7,16,17,18,19,20,21,22,23,32,33,34,35,36,37,38,39,48,49,..., dimensions={0} | all-to-all | bytes 6291456 | tf_op jit(solution)/shard_map/all_to_all | solution.py:408
  59.8 3.4 %read.1 = (bf16[128,1152]{1,0:T(8,128)(2,1)}, s32[8,256]{1,0:T(8,128)}, bf16[8,128,192]{2,1,0:T(8,128)(2,1)}, s32[32]{0:T(128)}) custom-call(bf16[1536,1024]{1,0:T(8,128)(2,1)} %bitcast.35), custom_call_target="tpu_custom_call" | custom-call | tf_op jit(solution)/shard_map/read/pallas_call | solution.py:434
  63.2 0.6 collective-permute-start.7
  63.9 5.8 %pack.1.packed_in = bf16[1536,1152]{1,0:T(8,128)(2,1)} custom-call(s32[32]{0:T(128)} %get-tuple-element.34.info, bf16[1536,1024]{1,0:T(8,128)(2,1)} %bitcast.36, s32[8,256]{1,0:T(8,128)} %get-tuple-element.36.spots, bf16[8,128,192]{2,1,0:T(8,128)(2,1)} %get-tuple-element.37.fields), custom_call_target="tpu_custom_call" | custom-call | flops 736100352 | bytes 7077888 | tf_op jit(solution)/shard_map/pack/pallas_call | solution.py:460
  69.7 1.1 collective-permute-done.7.near
  70.7 0.0 copy-start
  70.8 0.7 copy-done
  71.5 1.7 %append.1 = (bf16[1536,1152]{1,0:T(8,128)(2,1)}, s32[32]{0:T(128)}) custom-call(s32[32]{0:T(128)} %get-tuple-element.34.info, bf16[128,1152]{1,0:T(8,128)(2,1)} %copy-done, bf16[1536,1152]{1,0:T(8,128)(2,1)} %pack.1.packed_in), custom_call_target="tpu_custom_call", output_to_operand_aliasing={{0}: (2, {})} | custom-call | tf_op jit(solution)/shard_map/append/pallas_call | solution.py:477
  73.2 0.1 collective-permute-start.9
  73.3 0.5 collective-permute-start.8
  73.8 4.1 %own.1.best_in = f32[1,1536]{1,0:T(1,128)} custom-call(s32[32]{0:T(128)} %get-tuple-element.38.info, bf16[1536,1152]{1,0:T(8,128)(2,1)} %get-tuple-element.39.packed), custom_call_target="tpu_custom_call" | custom-call | flops 2147483648 | bytes 3538944 | tf_op jit(solution)/shard_map/own/pallas_call | solution.py:494
  77.9 0.0 copy-start.2
  78.0 0.0 copy-start.3
  78.0 0.0 copy-start.4
  78.0 1.4 %collective-permute-done.8.other_info = s32[32]{0:T(128)S(1)} collective-permute-done((s32[32]{0:T(128)}, s32[32]{0:T(128)S(1)}, u32[]{:S(2)}, u32[]{:S(2)}) %collective-permute-start.8) | collective-permute-done | bytes 160 | tf_op jit(solution)/shard_map/ppermute | solution.py:492
  79.3 0.0 copy-start.5
  79.3 0.5 collective-permute-done.9.other
  79.9 0.1 copy-done.5
  79.9 5.6 %other.1 = f32[64,128]{1,0:T(8,128)} custom-call(s32[32]{0:T(128)} %get-tuple-element.38.info, s32[32]{0:T(128)} %copy-done.5, bf16[1536,1152]{1,0:T(8,128)(2,1)} %get-tuple-element.39.packed, bf16[1536,1152]{1,0:T(8,128)(2,1)} %collective-permute-done.9.other, bf16[128,1152]{1,0:T(8,128)(2,1)} %copy-done, f32[1,1536]{1,0:T(1,128)} %own.1.best_in, ...), custom_call_target="tpu_custom_call" | custom-call | tf_op jit(solution)/shard_map/other/pallas_call | solution.py:510
  85.5 16.7 %all-to-all-start.3 = ((f32[64,1,128]{2,1,0:T(1,128)}), f32[64,1,128]{2,1,0:T(1,128)S(1)}, u32[]{:S(2)}, u32[]{:S(2)}) async-start(f32[64,1,128]{2,1,0:T(1,128)} %bitcast.39), calls=%async_computation.3 | async-start | bytes 65536 | tf_op jit(solution)/shard_map/all_to_all | solution.py:408
  102.2 9.6 %all-to-all-done.3 = f32[64,1,128]{2,1,0:T(1,128)S(1)} async-done(((f32[64,1,128]{2,1,0:T(1,128)}), f32[64,1,128]{2,1,0:T(1,128)S(1)}, u32[]{:S(2)}, u32[]{:S(2)}) %all-to-all-start.3) | async-done | bytes 32800 | tf_op jit(solution)/shard_map/all_to_all | solution.py:408
  111.7 0.0 copy-start.1
  111.7 0.6 copy-done.1
  112.3 1.5 %home.1 = (f32[1,512]{1,0:T(1,128)S(1)}, s32[1]{0:T(128)}) custom-call(s32[1]{0:T(128)} %bitcast.9.me, f32[64,128]{1,0:T(8,128)} %bitcast.40, s32[8,512]{1,0:T(8,128)} %get-tuple-element.40.place), custom_call_target="tpu_custom_call" | custom-call | tf_op jit(solution)/shard_map/home/pallas_call | solution.py:528
  114.5 0.0 copy-done.2
  114.5 0.0 copy-done.3
  114.5 0.0 copy-done.4
  114.6 0.3 conditional.1
  114.8 0.0 copy-start.6
  114.8 0.6 copy-done.6
Async XLA Ops:
  63.2 7.5 %collective-permute-start.7 = (bf16[128,1152]{1,0:T(8,128)(2,1)}, bf16[128,1152]{1,0:T(8,128)(2,1)S(1)}, u32[]{:S(2)}, u32[]{:S(2)}) collective-permute-start(bf16[128,1152]{1,0:T(8,128)(2,1)} %get-tuple-element.35), channel_id=1, source_target_pairs={{0,1},{1,0},{2,3},{3,2},{4,5},{5,4},{6,7},{7,6},{8,9},{9,8},{10,11... | collective-permute-start | bytes 884744 | tf_op jit(solution)/shard_map/ppermute | solution.py:459
  70.7 0.7 copy-start
  73.2 6.6 %collective-permute-start.9 = (bf16[1536,1152]{1,0:T(8,128)(2,1)}, bf16[1536,1152]{1,0:T(8,128)(2,1)}, u32[]{:S(2)}, u32[]{:S(2)}) collective-permute-start(bf16[1536,1152]{1,0:T(8,128)(2,1)} %get-tuple-element.39.packed), channel_id=1, source_target_pairs={{0,8},{8,0},{16,24},{24,16},{32,40},{40,32},{48,56},{56,48},{64,72... | collective-permute-start | bytes 10616840 | tf_op jit(solution)/shard_map/ppermute | solution.py:493
  73.3 6.0 %collective-permute-start.8 = (s32[32]{0:T(128)}, s32[32]{0:T(128)S(1)}, u32[]{:S(2)}, u32[]{:S(2)}) collective-permute-start(s32[32]{0:T(128)} %get-tuple-element.38.info), channel_id=1, source_target_pairs={{0,8},{8,0},{16,24},{24,16},{32,40},{40,32},{48,56},{56,48},{64,72... | collective-permute-start | bytes 392 | tf_op jit(solution)/shard_map/ppermute | solution.py:492
  77.9 36.6 %copy-start.2 = (s32[512,1]{0,1:T(1,128)S(1)}, s32[512,1]{0,1:T(1,128)}, u32[]{:S(2)}) copy-start(s32[512,1]{0,1:T(1,128)} %param.7) | copy-start | bytes 6148
  78.0 36.6 %copy-start.3 = (s32[512]{0:T(512)S(1)}, s32[512]{0:T(512)}, u32[]{:S(2)}) copy-start(s32[512]{0:T(512)} %param.8) | copy-start | bytes 6148
  78.0 36.6 %copy-start.4 = (s32[512]{0:T(512)S(1)}, s32[512]{0:T(512)}, u32[]{:S(2)}) copy-start(s32[512]{0:T(512)} %param.9) | copy-start | bytes 6148
  79.3 0.6 copy-start.5
  85.5 26.2 %all-to-all-start.3 = ((f32[64,1,128]{2,1,0:T(1,128)}), f32[64,1,128]{2,1,0:T(1,128)S(1)}, u32[]{:S(2)}, u32[]{:S(2)}) async-start(f32[64,1,128]{2,1,0:T(1,128)} %bitcast.39), calls=%async_computation.3 | async-start | bytes 65536 | tf_op jit(solution)/shard_map/all_to_all | solution.py:408
  111.7 0.6 copy-start.1
  114.8 0.6 copy-start.6

commit v3 on v2

--- a/solution.py
+++ b/solution.py
@@ -25,6 +25,7 @@
 F32 = jnp.float32
 BF16 = jnp.bfloat16
 I32 = jnp.int32
+LOWEST = -(2**31)
 
 
 def iota(shape, dim):
@@ -99,7 +100,8 @@
 
     pick = hot(iota((block, rows), 0) == slot[...] - step * block)
     moved = dot(pick, unit[...])
-    end = ends[pl.ds(pl.multiple_of(step * 8, 8), 8), :]
+    senders = block // BLOCK
+    end = ends[pl.ds(pl.multiple_of(step * senders, 8), senders), :]
     last = iota((8, width), 0) == 7
     pieces = []
     for at in range(block // BLOCK):
@@ -197,6 +199,12 @@
     tiles = info[16]
     room[0:16, :] = jnp.zeros((16, room.shape[1]), BF16)
     first = jnp.int32(0)
+    done = jnp.int32(0)
+
+    def put(at):
+        rows = pl.ds(pl.multiple_of(at * TILE, TILE), TILE)
+        return pltpu.make_async_copy(room.at[rows, :], packed.at[rows, :], placed.at[at])
+
     for at in range(chunks):
         first = pl.multiple_of(jnp.minimum(info[at], ROOM - WINDOW), 16)
         spot = spots[at : at + 1, 0:CHUNK] - first
@@ -207,17 +215,20 @@
         for span, value in ((pl.ds(0, width), rows_in), (pl.ds(width, EXTRA), side)):
             room[here, span] = (room[here, span].astype(F32) + value[:16]).astype(BF16)
             room[after, span] = value[16:].astype(BF16)
+        if at + 1 < chunks:
+            filled = info[at + 1] // TILE
+            pl.when(filled > done)(put(done).start)
+            done = filled
 
     def clear(at, carry):
         room[pl.ds(pl.multiple_of(at * 16, 16), 16), :] = jnp.zeros((16, room.shape[1]), BF16)
         return carry
 
     lax.fori_loop((first + WINDOW) // 16, tiles * (TILE // 16), clear, 0)
-    for wait in (False, True):
-        for at in range(TILES):
-            rows = pl.ds(at * TILE, TILE)
-            copy = pltpu.make_async_copy(room.at[rows, :], packed.at[rows, :], placed.at[at])
-            pl.when(at < tiles)(copy.wait if wait else copy.start)
+    for at in range(TILES):
+        pl.when((at >= done) & (at < tiles))(put(at).start)
+    for at in range(TILES):
+        pl.when(at < tiles)(put(at).wait)
 
 
 def append_kernel(info, near, packed_in, packed, info_out, window, blank, sems):
@@ -269,15 +280,18 @@
         put.wait()
 
 
-def score(queries, low, high, keys, key_tiles, best, marks):
+def score(queries, query_tiles, keys, key_tiles, best, marks, bounds):
     width = queries.shape[1] - EXTRA
+    fields = fields_of(queries[:, width:]).astype(I32)
+    bounds[0:1, :] = (fields[1:2, :] * 128 + fields[0:1, :] + fields[4:5, :]) * 65536
+    bounds[1:2, :] = fields[2:3, :] * 256 + fields[3:4, :] + LOWEST
 
     def mark_step(at, carry):
         span = pl.ds(pl.multiple_of(at * TILE, TILE), TILE)
         side = keys[span, width:].astype(F32).astype(I32)
         mark = (side[:, 1:2] * 128 + side[:, 0:1] + side[:, 4:5]) * 65536
-        mark = mark + side[:, 2:3] * 256 + side[:, 3:4]
-        marks[span, :] = jnp.broadcast_to(mark, (TILE, TILE))
+        mark = mark + side[:, 2:3] * 256 + side[:, 3:4] + LOWEST
+        marks[span, :] = jnp.broadcast_to(mark, (TILE, EXTRA))
         return carry
 
     lax.fori_loop(0, key_tiles, mark_step, 0)
@@ -285,17 +299,15 @@
     def against(size):
         def query_step(at, carry):
             rows = pl.ds(pl.multiple_of(at * TILE, TILE), TILE)
-            fields = fields_of(queries[rows, width:]).astype(I32)
-            cluster = (fields[1:2, :] * 128 + fields[0:1, :] + fields[4:5, :]) * 65536
-            upper = cluster + fields[2:3, :] * 256 + fields[3:4, :]
             mark = marks[:size, :]
+            mark = jnp.concatenate([mark] * (TILE // EXTRA), 1)
             scores = dot(keys[:size, :width], queries[rows, :width], COLS)
-            earlier = (mark >= cluster) & (mark < upper)
+            earlier = mark - bounds[0:1, rows] < bounds[1:2, rows]
             found = jnp.max(jnp.where(earlier, scores, -1.0), 0, keepdims=True)
             best[:, rows] = jnp.maximum(best[:, rows], found)
             return carry
 
-        lax.fori_loop(low, high, query_step, 0)
+        lax.fori_loop(0, query_tiles, query_step, 0)
 
     if isinstance(key_tiles, int):
         against(key_tiles * TILE)
@@ -318,16 +330,16 @@
         pl.when(at < tiles)(copy.wait)
 
 
-def own_kernel(info, packed, best, mine, marks, sems):
+def own_kernel(info, packed, best, mine, marks, bounds, sems):
     fetch(packed, mine, info[16], sems)
     best[...] = jnp.full(best.shape, -1.0, F32)
     fetched(packed, mine, info[16], sems)
-    score(mine, 0, info[16], mine, info[16], best, marks)
+    score(mine, info[16], mine, info[16], best, marks, bounds)
 
 
 def other_kernel(
     info, other_info, packed, other, near, best_in, spots, back,
-    mine, theirs, best, marks, sems, other_sems,
+    mine, theirs, best, split, marks, bounds, sems, other_sems,
 ):
     tiles, other_tiles = info[16], other_info[16]
     fetch(packed, mine, tiles, sems)
@@ -336,17 +348,17 @@
     best[:, PACKED:] = jnp.full((1, best.shape[1] - PACKED), -1.0, F32)
     fetched(packed, mine, tiles, sems)
     fetched(other, theirs, other_tiles, other_sems)
-    score(mine, 0, tiles, theirs, other_tiles, best, marks)
+    score(mine, tiles, theirs, other_tiles, best, marks, bounds)
     flag = jnp.maximum(info[17], other_info[17]).astype(F32)
     reach = 384
-    row = iota((16, reach), 0)
+    row = iota((16, best.shape[1]), 0)
+    stack = jnp.zeros(row.shape, F32)
+    for at, part in enumerate(thirds(best[...])):
+        stack = jnp.where(row == at, part.astype(F32), stack)
+    split[...] = stack.astype(BF16)
 
     def stacked(first, count):
-        parts = thirds(best[:, pl.ds(pl.multiple_of(first, 128), count)])
-        stack = jnp.zeros((16, count), F32)
-        for at, part in enumerate(parts):
-            stack = jnp.where(row[:, :count] == at, part.astype(F32), stack)
-        return stack.astype(BF16)
+        return split[:, pl.ds(pl.multiple_of(first, 128), count)]
 
     sub, lane = iota((8, EXTRA), 0), iota((8, EXTRA), 1)
     lower = (lane >= sub * BLOCK) & (lane < sub * BLOCK + BLOCK)
@@ -398,6 +410,7 @@
 SCALARS = pl.BlockSpec(memory_space=pltpu.SMEM)
 PLACED = pl.BlockSpec(memory_space=pl.ANY)
 PARAMS = pltpu.CompilerParams(vmem_limit_bytes=63 * 1024 * 1024)
+LESS = pltpu.CompilerParams(vmem_limit_bytes=28 * 1024 * 1024)
 
 
 def array(shape, dtype):
@@ -418,9 +431,9 @@
     me = ((lax.axis_index("grp") >> 1) * 8 + lax.axis_index("blk")).astype(I32).reshape(1)
     sent, place = pl.pallas_call(
         send_kernel,
-        grid=(chunks,),
+        grid=(chunks // 2,),
         in_specs=[SCALARS, whole((rows, width))] + [whole((1, rows))] * 3,
-        out_specs=[pl.BlockSpec((CHUNK, width), lambda i: (i, 0)), whole((8, rows))],
+        out_specs=[pl.BlockSpec((2 * CHUNK, width), lambda i: (i, 0)), whole((8, rows))],
         out_shape=[array((lines, width), BF16), array((8, rows), I32)],
         scratch_shapes=[
             pltpu.VMEM((rows, width), BF16),
@@ -485,7 +498,7 @@
             pltpu.SemaphoreType.DMA((3,)),
         ],
         input_output_aliases={2: 0},
-        compiler_params=PARAMS,
+        compiler_params=LESS,
         name="append",
     )(info, near, packed)
     swap = [(i, i ^ 1) for i in range(16)]
@@ -498,10 +511,11 @@
         out_shape=array((1, PACKED), F32),
         scratch_shapes=[
             pltpu.VMEM((PACKED, full), BF16),
-            pltpu.VMEM((PACKED, TILE), I32),
+            pltpu.VMEM((PACKED, EXTRA), I32),
+            pltpu.VMEM((8, PACKED), I32),
             pltpu.SemaphoreType.DMA((TILES,)),
         ],
-        compiler_params=PARAMS,
+        compiler_params=LESS,
         cost_estimate=pl.CostEstimate(
             flops=2 * 1024 * 1024 * width, bytes_accessed=2 * PACKED * full, transcendentals=0
         ),
@@ -517,11 +531,13 @@
             pltpu.VMEM((PACKED, full), BF16),
             pltpu.VMEM((PACKED, full), BF16),
             pltpu.VMEM((1, PACKED + 2 * TILE), F32),
-            pltpu.VMEM((PACKED, TILE), I32),
+            pltpu.VMEM((16, PACKED + 2 * TILE), BF16),
+            pltpu.VMEM((PACKED, EXTRA), I32),
+            pltpu.VMEM((8, PACKED), I32),
             pltpu.SemaphoreType.DMA((TILES,)),
             pltpu.SemaphoreType.DMA((TILES,)),
         ],
-        compiler_params=PARAMS,
+        compiler_params=LESS,
         name="other",
     )(info, other_info, packed, other, near, best, spots)
     home = exchange(back)
@@ -530,16 +546,16 @@
         in_specs=[SCALARS, whole((CHIPS, EXTRA)), whole((8, rows))],
         out_specs=[whole((1, rows)), SCALARS],
         out_shape=[array((1, rows), F32), array((1,), I32)],
-        compiler_params=PARAMS,
+        compiler_params=LESS,
         name="home",
     )(me, home, place)
     return highest.reshape(rows), flag[0]
 
 
-def group_kernel(queries, keys, best_in, best, marks):
+def group_kernel(queries, keys, best_in, best, marks, bounds):
     best[...] = best_in[...]
     tiles = keys.shape[0] // TILE
-    score(queries, 0, tiles, keys, tiles, best, marks)
+    score(queries, tiles, keys, tiles, best, marks, bounds)
 
 
 def by_group(embed, owner, local_id, rank):
@@ -568,7 +584,7 @@
             in_specs=[whole((width, full))] * 2 + [whole((1, width))],
             out_specs=whole((1, width)),
             out_shape=array((1, width), F32),
-            scratch_shapes=[pltpu.VMEM((width, TILE), I32)],
+            scratch_shapes=[pltpu.VMEM((width, EXTRA), I32), pltpu.VMEM((8, width), I32)],
             compiler_params=PARAMS,
             name="group",
         )(routed, lax.ppermute(routed, "blk", turn) if by else routed, best)

time: 117 us -> 111 us (0.949); the launches traced: 115 us -> 113 us
  Pallas kernels: 29 us -> 25 us
  starting transfers between devices: 17.9 us -> 20.2 us
  local copies, waits for them, and re-layouts: 1.99 us -> 0.61 us
    all_to_all x1, starting transfers between devices: 16.7 us -> 19 us  [exchange(): lax.all_to_all(x, BOTH, split_axis=0, concat_axis=0, tiled=True, axis_ind...]
    pallas_call x1, Pallas kernels: 6.81 us -> 5.33 us  [direct(): pl.pallas_call(send_kernel, grid=(chunks // 2,), in_specs=[SCALARS, whole...]
    unnamed x14 -> x16, local copies, waits for them, and re-layouts: 1.99 us -> 0.61 us
  transfers between devices with their start and end apart: 4 -> 4, of which waited for: 4 -> 4; matrix products, arithmetic and copies ran while one was open for 0% -> 0% of each run, Pallas kernels for 9% -> 8%
where the time goes in v3:
time: 111 us; the launch traced here: 113 us
  blocking collectives  53 us (48%)
  Pallas kernels  25 us (23%)
  starting transfers between devices  20.2 us (18%)
  waiting for transfers between devices  13.1 us (12%)
    all_to_all x1, blocking collectives, exchange(): lax.all_to_all(x, BOTH, split_axis=0, concat_axis=0, tiled=True, axis_ind...  53 us
    all_to_all x1, starting transfers between devices, exchange(): lax.all_to_all(x, BOTH, split_axis=0, concat_axis=0, tiled=True, axis_ind...  19 us
    all_to_all x1, waiting for transfers between devices, exchange(): lax.all_to_all(x, BOTH, split_axis=0, concat_axis=0, tiled=True, axis_ind...  9.55 us
    pallas_call x1, Pallas kernels, direct(): pl.pallas_call(pack_kernel, in_specs=[SCALARS, PLACED, whole((chunks, 2 *...  5.62 us
    pallas_call x1, Pallas kernels, direct(): pl.pallas_call(send_kernel, grid=(chunks // 2,), in_specs=[SCALARS, whole...  5.33 us
    pallas_call x1, Pallas kernels, direct(): pl.pallas_call(other_kernel, in_specs=[SCALARS, SCALARS, PLACED, PLACED]...  4.96 us
    pallas_call x1, Pallas kernels, direct(): pl.pallas_call(own_kernel, in_specs=[SCALARS, PLACED], out_specs=whole((1...  3.6 us
    pallas_call x1, Pallas kernels, direct(): pl.pallas_call(read_kernel, in_specs=[PLACED], out_specs=[whole((SPILL, f...  3.43 us
  transfers between devices with their start and end apart: 4, of which 4 were waited for; matrix products, arithmetic and copies ran while one was open for 0% of the time, Pallas kernels for 8%

profile of v3, /device:TPU:0, one launch (start us, length us, event | category | flops | bytes accessed | tf_op | source)
XLA Modules:
  0.0 112.9 jit_solution(7458906085791182177)
XLA Ops:
  0.0 5.3 %send.1 = (bf16[1536,1024]{1,0:T(8,128)(2,1)}, s32[8,512]{1,0:T(8,128)}) custom-call(s32[1]{0:T(128)} %bitcast.9.me, bf16[512,1024]{1,0:T(8,128)(2,1)} %embed.1, s32[1,512]{1,0:T(1,128)} %bitcast.40, s32[1,512]{1,0:T(1,128)} %bitcast.43, s32[1,512]{1,0:T(1,128)} %bitcast.44), custom_call_target="tpu_custom_call" | custom-call | tf_op jit(solution)/shard_map/send/pallas_call | solution.py:432
  5.3 53.0 %all_to_all.28 = bf16[64,24,1024]{2,1,0:T(8,128)(2,1)} all-to-all(bf16[64,24,1024]{2,1,0:T(8,128)(2,1)} %bitcast.39), channel_id=1, replica_groups={{0,1,2,3,4,5,6,7,16,17,18,19,20,21,22,23,32,33,34,35,36,37,38,39,48,49,..., dimensions={0} | all-to-all | bytes 6291456 | tf_op jit(solution)/shard_map/all_to_all | solution.py:421
  58.3 3.4 %read.1 = (bf16[128,1152]{1,0:T(8,128)(2,1)}, s32[8,256]{1,0:T(8,128)}, bf16[8,128,192]{2,1,0:T(8,128)(2,1)}, s32[32]{0:T(128)}) custom-call(bf16[1536,1024]{1,0:T(8,128)(2,1)} %bitcast.36), custom_call_target="tpu_custom_call" | custom-call | tf_op jit(solution)/shard_map/read/pallas_call | solution.py:447
  61.7 0.7 collective-permute-start.7
  62.4 0.0 copy-start.2
  62.4 5.6 %pack.1.packed_in = bf16[1536,1152]{1,0:T(8,128)(2,1)} custom-call(s32[32]{0:T(128)} %get-tuple-element.34.info, bf16[1536,1024]{1,0:T(8,128)(2,1)} %bitcast.37, s32[8,256]{1,0:T(8,128)} %get-tuple-element.36.spots, bf16[8,128,192]{2,1,0:T(8,128)(2,1)} %get-tuple-element.37.fields), custom_call_target="tpu_custom_call" | custom-call | flops 736100352 | bytes 7077888 | tf_op jit(solution)/shard_map/pack/pallas_call | solution.py:473
  68.0 1.3 %collective-permute-done.7.near = bf16[128,1152]{1,0:T(8,128)(2,1)S(1)} collective-permute-done((bf16[128,1152]{1,0:T(8,128)(2,1)}, bf16[128,1152]{1,0:T(8,128)(2,1)S(1)}, u32[]{:S(2)}, u32[]{:S(2)}) %collective-permute-start.7) | collective-permute-done | bytes 294944 | tf_op jit(solution)/shard_map/ppermute | solution.py:472
  69.3 0.0 copy-done.2
  69.3 1.4 %append.1 = (bf16[1536,1152]{1,0:T(8,128)(2,1)}, s32[32]{0:T(128)S(1)}) custom-call(s32[32]{0:T(128)S(1)} %copy-done.2, bf16[128,1152]{1,0:T(8,128)(2,1)S(1)} %collective-permute-done.7.near, bf16[1536,1152]{1,0:T(8,128)(2,1)} %pack.1.packed_in), custom_call_target="tpu_custom_call", output_to_operand_aliasing={{0}: (2, {})} | custom-call | tf_op jit(solution)/shard_map/append/pallas_call | solution.py:490
  70.6 0.1 collective-permute-start.9
  70.7 0.0 copy-start
  70.8 0.5 collective-permute-start.8
  71.2 3.6 %own.1.best_in = f32[1,1536]{1,0:T(1,128)S(1)} custom-call(s32[32]{0:T(128)S(1)} %get-tuple-element.38.info, bf16[1536,1152]{1,0:T(8,128)(2,1)} %get-tuple-element.39.packed), custom_call_target="tpu_custom_call" | custom-call | flops 2147483648 | bytes 3538944 | tf_op jit(solution)/shard_map/own/pallas_call | solution.py:507
  74.8 0.0 copy-start.1
  74.9 0.0 copy-start.3
  74.9 0.0 copy-start.4
  74.9 0.0 copy-start.5
  74.9 0.0 copy-start.6
  74.9 1.7 %collective-permute-done.8.other_info = s32[32]{0:T(128)S(1)} collective-permute-done((s32[32]{0:T(128)S(1)}, s32[32]{0:T(128)S(1)}, u32[]{:S(2)}, u32[]{:S(2)}) %collective-permute-start.8) | collective-permute-done | bytes 160 | tf_op jit(solution)/shard_map/ppermute | solution.py:505
  76.6 0.6 collective-permute-done.9.other
  77.2 0.0 copy-done
  77.2 5.0 %other.1 = f32[64,128]{1,0:T(8,128)} custom-call(s32[32]{0:T(128)S(1)} %get-tuple-element.38.info, s32[32]{0:T(128)S(1)} %collective-permute-done.8.other_info, bf16[1536,1152]{1,0:T(8,128)(2,1)} %get-tuple-element.39.packed, bf16[1536,1152]{1,0:T(8,128)(2,1)S(1)} %collective-permute-done.9.other, bf16[128,1152]{1,0:T(8,128)(2,1)S(1)} %collective-permute-done.7.near, ...), custom_call_target="tpu_custom_call" | custom-call | tf_op jit(solution)/shard_map/other/pallas_call | solution.py:524
  82.1 19.0 %all-to-all-start.3 = ((f32[64,1,128]{2,1,0:T(1,128)}), f32[64,1,128]{2,1,0:T(1,128)S(1)}, u32[]{:S(2)}, u32[]{:S(2)}) async-start(f32[64,1,128]{2,1,0:T(1,128)} %bitcast.16), calls=%async_computation.3 | async-start | bytes 65536 | tf_op jit(solution)/shard_map/all_to_all | solution.py:421
  101.1 9.6 %all-to-all-done.3 = f32[64,1,128]{2,1,0:T(1,128)S(1)} async-done(((f32[64,1,128]{2,1,0:T(1,128)}), f32[64,1,128]{2,1,0:T(1,128)S(1)}, u32[]{:S(2)}, u32[]{:S(2)}) %all-to-all-start.3) | async-done | bytes 32800 | tf_op jit(solution)/shard_map/all_to_all | solution.py:421
  110.7 0.0 copy-done.1
  110.7 0.7 home.1
  112.0 0.0 copy-done.3
  112.0 0.0 copy-done.4
  112.0 0.0 copy-done.5
  112.0 0.0 copy-done.6
  112.0 0.3 conditional.1
  112.3 0.0 copy-start.7
  112.3 0.6 copy-done.7
Async XLA Ops:
  61.7 7.5 %collective-permute-start.7 = (bf16[128,1152]{1,0:T(8,128)(2,1)}, bf16[128,1152]{1,0:T(8,128)(2,1)S(1)}, u32[]{:S(2)}, u32[]{:S(2)}) collective-permute-start(bf16[128,1152]{1,0:T(8,128)(2,1)} %get-tuple-element.35), channel_id=1, source_target_pairs={{0,1},{1,0},{2,3},{3,2},{4,5},{5,4},{6,7},{7,6},{8,9},{9,8},{10,11... | collective-permute-start | bytes 884744 | tf_op jit(solution)/shard_map/ppermute | solution.py:472
  62.4 6.9 %copy-start.2 = (s32[32]{0:T(128)S(1)}, s32[32]{0:T(128)}, u32[]{:S(2)}) copy-start(s32[32]{0:T(128)} %get-tuple-element.34.info) | copy-start | bytes 388
  70.6 6.5 %collective-permute-start.9 = (bf16[1536,1152]{1,0:T(8,128)(2,1)}, bf16[1536,1152]{1,0:T(8,128)(2,1)S(1)}, u32[]{:S(2)}, u32[]{:S(2)}) collective-permute-start(bf16[1536,1152]{1,0:T(8,128)(2,1)} %get-tuple-element.39.packed), channel_id=1, source_target_pairs={{0,8},{8,0},{16,24},{24,16},{32,40},{40,32},{48,56},{56,48},{64,72... | collective-permute-start | bytes 10616840 | tf_op jit(solution)/shard_map/ppermute | solution.py:506
  70.7 6.4 %copy-start = (s32[8,256]{1,0:T(8,128)S(1)}, s32[8,256]{1,0:T(8,128)}, u32[]{:S(2)}) copy-start(s32[8,256]{1,0:T(8,128)} %get-tuple-element.36.spots) | copy-start | bytes 24580
  70.8 5.8 %collective-permute-start.8 = (s32[32]{0:T(128)S(1)}, s32[32]{0:T(128)S(1)}, u32[]{:S(2)}, u32[]{:S(2)}) collective-permute-start(s32[32]{0:T(128)S(1)} %get-tuple-element.38.info), channel_id=1, source_target_pairs={{0,8},{8,0},{16,24},{24,16},{32,40},{40,32},{48,56},{56,48},{64,72... | collective-permute-start | bytes 392 | tf_op jit(solution)/shard_map/ppermute | solution.py:505
  74.8 35.8 %copy-start.1 = (s32[8,512]{1,0:T(8,128)S(1)}, s32[8,512]{1,0:T(8,128)}, u32[]{:S(2)}) copy-start(s32[8,512]{1,0:T(8,128)} %get-tuple-element.40.place) | copy-start | bytes 49156
  74.9 37.1 %copy-start.3 = (bf16[512,1024]{1,0:T(8,128)(2,1)S(1)}, bf16[512,1024]{1,0:T(8,128)(2,1)}, u32[]{:S(2)}) copy-start(bf16[512,1024]{1,0:T(8,128)(2,1)} %embed.1) | copy-start | bytes 3145732
  74.9 37.1 %copy-start.4 = (s32[512,1]{0,1:T(1,128)S(1)}, s32[512,1]{0,1:T(1,128)}, u32[]{:S(2)}) copy-start(s32[512,1]{0,1:T(1,128)} %param.7) | copy-start | bytes 6148
  74.9 37.1 %copy-start.5 = (s32[512]{0:T(512)S(1)}, s32[512]{0:T(512)}, u32[]{:S(2)}) copy-start(s32[512]{0:T(512)} %param.8) | copy-start | bytes 6148
  74.9 37.1 %copy-start.6 = (s32[512]{0:T(512)S(1)}, s32[512]{0:T(512)}, u32[]{:S(2)}) copy-start(s32[512]{0:T(512)} %param.9) | copy-start | bytes 6148
  82.1 28.5 %all-to-all-start.3 = ((f32[64,1,128]{2,1,0:T(1,128)}), f32[64,1,128]{2,1,0:T(1,128)S(1)}, u32[]{:S(2)}, u32[]{:S(2)}) async-start(f32[64,1,128]{2,1,0:T(1,128)} %bitcast.16), calls=%async_computation.3 | async-start | bytes 65536 | tf_op jit(solution)/shard_map/all_to_all | solution.py:421
  112.3 0.6 copy-start.7

commit v4 on v3

--- a/solution.py
+++ b/solution.py
@@ -409,7 +409,7 @@
 
 SCALARS = pl.BlockSpec(memory_space=pltpu.SMEM)
 PLACED = pl.BlockSpec(memory_space=pl.ANY)
-PARAMS = pltpu.CompilerParams(vmem_limit_bytes=63 * 1024 * 1024)
+
 LESS = pltpu.CompilerParams(vmem_limit_bytes=28 * 1024 * 1024)
 
 
@@ -440,7 +440,7 @@
             pltpu.VMEM((1, rows), I32),
             pltpu.VMEM((CHIPS, width), F32),
         ],
-        compiler_params=PARAMS,
+        compiler_params=LESS,
         name="send",
     )(me, embed, owner.reshape(1, rows), local_id.reshape(1, rows), rank.reshape(1, rows))
     taken = exchange(sent.reshape(CHIPS, BLOCK, width)).reshape(lines, width)
@@ -466,7 +466,7 @@
             pltpu.VMEM((chunks, CHUNK), I32),
             pltpu.SemaphoreType.DMA((chunks,)),
         ],
-        compiler_params=PARAMS,
+        compiler_params=LESS,
         name="read",
     )(taken)
     near = lax.ppermute(spill, BOTH, [(i, i ^ 1) for i in range(2 * CHIPS)])
@@ -481,7 +481,7 @@
             pltpu.SemaphoreType.DMA((chunks,)),
             pltpu.SemaphoreType.DMA((TILES,)),
         ],
-        compiler_params=PARAMS,
+        compiler_params=LESS,
         cost_estimate=pl.CostEstimate(
             flops=2 * lines * WINDOW * full, bytes_accessed=4 * lines * full, transcendentals=0
         ),
@@ -585,7 +585,7 @@
             out_specs=whole((1, width)),
             out_shape=array((1, width), F32),
             scratch_shapes=[pltpu.VMEM((width, EXTRA), I32), pltpu.VMEM((8, width), I32)],
-            compiler_params=PARAMS,
+            compiler_params=LESS,
             name="group",
         )(routed, lax.ppermute(routed, "blk", turn) if by else routed, best)
     home = lax.all_to_all(

time: 111 us -> 103 us (0.928); the launches traced: 113 us -> 102 us
  starting transfers between devices: 20.2 us -> 12.8 us
  Pallas kernels: 25 us -> 21 us
    all_to_all x1, starting transfers between devices: 19 us -> 11.6 us  [exchange(): lax.all_to_all(x, BOTH, split_axis=0, concat_axis=0, tiled=True, axis_ind...]
    ppermute x1, waiting for transfers between devices: 1.68 us -> 3.02 us  [direct(): other_info = lax.ppermute(info, 'grp', swap)]
    pallas_call x1, Pallas kernels: 5.33 us -> 4.15 us  [direct(): pl.pallas_call(send_kernel, grid=(chunks // 2,), in_specs=[SCALARS, whole...]
  transfers between devices with their start and end apart: 4 -> 4, of which waited for: 4 -> 3; matrix products, arithmetic and copies ran while one was open for 0% -> 0% of each run, Pallas kernels for 8% -> 8%
where the time goes in v4:
time: 103 us; the launch traced here: 102 us
  blocking collectives  52.7 us (51%)
  Pallas kernels  21 us (20%)
  waiting for transfers between devices  14.2 us (14%)
  starting transfers between devices  12.8 us (12%)
    all_to_all x1, blocking collectives, exchange(): lax.all_to_all(x, BOTH, split_axis=0, concat_axis=0, tiled=True, axis_ind...  52.7 us
    all_to_all x1, starting transfers between devices, exchange(): lax.all_to_all(x, BOTH, split_axis=0, concat_axis=0, tiled=True, axis_ind...  11.6 us
    all_to_all x1, waiting for transfers between devices, exchange(): lax.all_to_all(x, BOTH, split_axis=0, concat_axis=0, tiled=True, axis_ind...  9.55 us
    pallas_call x1, Pallas kernels, direct(): pl.pallas_call(pack_kernel, in_specs=[SCALARS, PLACED, whole((chunks, 2 *...  5.06 us
    pallas_call x1, Pallas kernels, direct(): pl.pallas_call(other_kernel, in_specs=[SCALARS, SCALARS, PLACED, PLACED]...  4.26 us
    pallas_call x1, Pallas kernels, direct(): pl.pallas_call(send_kernel, grid=(chunks // 2,), in_specs=[SCALARS, whole...  4.15 us
    ppermute x1, waiting for transfers between devices, direct(): other_info = lax.ppermute(info, 'grp', swap)  3.02 us
    pallas_call x1, Pallas kernels, direct(): pl.pallas_call(read_kernel, in_specs=[PLACED], out_specs=[whole((SPILL, f...  2.81 us
  transfers between devices with their start and end apart: 4, of which 3 were waited for; matrix products, arithmetic and copies ran while one was open for 0% of the time, Pallas kernels for 8%

profile of v4, /device:TPU:0, one launch (start us, length us, event | category | flops | bytes accessed | tf_op | source)
XLA Modules:
  0.0 102.3 jit_solution(18340349309957167451)
XLA Ops:
  0.0 4.2 %send.1 = (bf16[1536,1024]{1,0:T(8,128)(2,1)S(1)}, s32[8,512]{1,0:T(8,128)S(1)}) custom-call(s32[1]{0:T(128)} %bitcast.9.me, bf16[512,1024]{1,0:T(8,128)(2,1)} %embed.1, s32[1,512]{1,0:T(1,128)} %bitcast.56, s32[1,512]{1,0:T(1,128)} %bitcast.59, s32[1,512]{1,0:T(1,128)} %bitcast.60), custom_call_target="tpu_custom_call" | custom-call | tf_op jit(solution)/shard_map/send/pallas_call | solution.py:432
  4.2 52.7 %all_to_all.28 = bf16[64,24,1024]{2,1,0:T(8,128)(2,1)S(1)} all-to-all(bf16[64,24,1024]{2,1,0:T(8,128)(2,1)S(1)} %bitcast.53), channel_id=1, replica_groups={{0,1,2,3,4,5,6,7,16,17,18,19,20,21,22,23,32,33,34,35,36,37,38,39,48,49,..., dimensions={0} | all-to-all | bytes 6291456 | tf_op jit(solution)/shard_map/all_to_all | solution.py:421
  56.8 2.8 %read.1 = (bf16[128,1152]{1,0:T(8,128)(2,1)S(1)}, s32[8,256]{1,0:T(8,128)S(1)}, bf16[8,128,192]{2,1,0:T(8,128)(2,1)S(1)}, s32[32]{0:T(128)S(1)}) custom-call(bf16[1536,1024]{1,0:T(8,128)(2,1)S(1)} %bitcast.51), custom_call_target="tpu_custom_call" | custom-call | tf_op jit(solution)/shard_map/read/pallas_call | solution.py:447
  59.6 0.7 collective-permute-start.7
  60.3 5.1 %pack.1.packed_in = bf16[1536,1152]{1,0:T(8,128)(2,1)S(1)} custom-call(s32[32]{0:T(128)S(1)} %get-tuple-element.34.info, bf16[1536,1024]{1,0:T(8,128)(2,1)S(1)} %bitcast.52, s32[8,256]{1,0:T(8,128)S(1)} %get-tuple-element.36.spots, bf16[8,128,192]{2,1,0:T(8,128)(2,1)S(1)} %get-tuple-element.37.fields), custom_call_target="tpu_custom_call" | custom-call | flops 736100352 | bytes 7077888 | tf_op jit(solution)/shard_map/pack/pallas_call | solution.py:473
  65.4 1.6 %collective-permute-done.7.near = bf16[128,1152]{1,0:T(8,128)(2,1)S(1)} collective-permute-done((bf16[128,1152]{1,0:T(8,128)(2,1)S(1)}, bf16[128,1152]{1,0:T(8,128)(2,1)S(1)}, u32[]{:S(2)}, u32[]{:S(2)}) %collective-permute-start.7) | collective-permute-done | bytes 294944 | tf_op jit(solution)/shard_map/ppermute | solution.py:472
  67.0 1.4 %append.1 = (bf16[1536,1152]{1,0:T(8,128)(2,1)S(1)}, s32[32]{0:T(128)S(1)}) custom-call(s32[32]{0:T(128)S(1)} %get-tuple-element.34.info, bf16[128,1152]{1,0:T(8,128)(2,1)S(1)} %collective-permute-done.7.near, bf16[1536,1152]{1,0:T(8,128)(2,1)S(1)} %pack.1.packed_in), custom_call_target="tpu_custom_call", output_to_operand_aliasing={{0}: (2, {})} | custom-call | tf_op jit(solution)/shard_map/append/pallas_call | solution.py:490
  68.3 0.1 collective-permute-start.9
  68.4 0.5 collective-permute-start.8
  68.9 2.6 %own.1.best_in = f32[1,1536]{1,0:T(1,128)S(1)} custom-call(s32[32]{0:T(128)S(1)} %get-tuple-element.38.info, bf16[1536,1152]{1,0:T(8,128)(2,1)S(1)} %get-tuple-element.39.packed), custom_call_target="tpu_custom_call" | custom-call | flops 2147483648 | bytes 3538944 | tf_op jit(solution)/shard_map/own/pallas_call | solution.py:507
  71.6 0.0 copy-start
  71.6 0.0 copy-start.1
  71.6 0.0 copy-start.2
  71.6 0.0 copy-start.3
  71.6 3.0 %collective-permute-done.8.other_info = s32[32]{0:T(128)S(1)} collective-permute-done((s32[32]{0:T(128)S(1)}, s32[32]{0:T(128)S(1)}, u32[]{:S(2)}, u32[]{:S(2)}) %collective-permute-start.8) | collective-permute-done | bytes 160 | tf_op jit(solution)/shard_map/ppermute | solution.py:505
  74.6 0.0 collective-permute-done.9.other
  74.6 4.3 %other.1 = f32[64,128]{1,0:T(8,128)} custom-call(s32[32]{0:T(128)S(1)} %get-tuple-element.38.info, s32[32]{0:T(128)S(1)} %collective-permute-done.8.other_info, bf16[1536,1152]{1,0:T(8,128)(2,1)S(1)} %get-tuple-element.39.packed, bf16[1536,1152]{1,0:T(8,128)(2,1)S(1)} %collective-permute-done.9.other, bf16[128,1152]{1,0:T(8,128)(2,1)S(1)} %collective-permute-done.7.near, ...), custom_call_target="tpu_custom_call" | custom-call | tf_op jit(solution)/shard_map/other/pallas_call | solution.py:524
  78.9 11.6 %all-to-all-start.3 = ((f32[64,1,128]{2,1,0:T(1,128)}), f32[64,1,128]{2,1,0:T(1,128)S(1)}, u32[]{:S(2)}, u32[]{:S(2)}) async-start(f32[64,1,128]{2,1,0:T(1,128)} %bitcast.16), calls=%async_computation.3 | async-start | bytes 65536 | tf_op jit(solution)/shard_map/all_to_all | solution.py:421
  90.5 9.6 %all-to-all-done.3 = f32[64,1,128]{2,1,0:T(1,128)S(1)} async-done(((f32[64,1,128]{2,1,0:T(1,128)}), f32[64,1,128]{2,1,0:T(1,128)S(1)}, u32[]{:S(2)}, u32[]{:S(2)}) %all-to-all-start.3) | async-done | bytes 32800 | tf_op jit(solution)/shard_map/all_to_all | solution.py:421
  100.1 0.7 home.1
  101.4 0.0 copy-done
  101.4 0.0 copy-done.1
  101.4 0.0 copy-done.2
  101.5 0.0 copy-done.3
  101.5 0.3 conditional.1
  101.7 0.0 copy-start.4
  101.8 0.6 copy-done.4
Async XLA Ops:
  59.6 7.3 %collective-permute-start.7 = (bf16[128,1152]{1,0:T(8,128)(2,1)S(1)}, bf16[128,1152]{1,0:T(8,128)(2,1)S(1)}, u32[]{:S(2)}, u32[]{:S(2)}) collective-permute-start(bf16[128,1152]{1,0:T(8,128)(2,1)S(1)} %get-tuple-element.35), channel_id=1, source_target_pairs={{0,1},{1,0},{2,3},{3,2},{4,5},{5,4},{6,7},{7,6},{8,9},{9,8},{10,11... | collective-permute-start | bytes 884744 | tf_op jit(solution)/shard_map/ppermute | solution.py:472
  68.3 6.3 %collective-permute-start.9 = (bf16[1536,1152]{1,0:T(8,128)(2,1)S(1)}, bf16[1536,1152]{1,0:T(8,128)(2,1)S(1)}, u32[]{:S(2)}, u32[]{:S(2)}) collective-permute-start(bf16[1536,1152]{1,0:T(8,128)(2,1)S(1)} %get-tuple-element.39.packed), channel_id=1, source_target_pairs={{0,8},{8,0},{16,24},{24,16},{32,40},{40,32},{48,56},{56,48},{64,72... | collective-permute-start | bytes 10616840 | tf_op jit(solution)/shard_map/ppermute | solution.py:506
  68.4 6.2 %collective-permute-start.8 = (s32[32]{0:T(128)S(1)}, s32[32]{0:T(128)S(1)}, u32[]{:S(2)}, u32[]{:S(2)}) collective-permute-start(s32[32]{0:T(128)S(1)} %get-tuple-element.38.info), channel_id=1, source_target_pairs={{0,8},{8,0},{16,24},{24,16},{32,40},{40,32},{48,56},{56,48},{64,72... | collective-permute-start | bytes 392 | tf_op jit(solution)/shard_map/ppermute | solution.py:505
  71.6 29.9 %copy-start = (bf16[512,1024]{1,0:T(8,128)(2,1)S(1)}, bf16[512,1024]{1,0:T(8,128)(2,1)}, u32[]{:S(2)}) copy-start(bf16[512,1024]{1,0:T(8,128)(2,1)} %embed.1) | copy-start | bytes 3145732
  71.6 29.9 %copy-start.1 = (s32[512,1]{0,1:T(1,128)S(1)}, s32[512,1]{0,1:T(1,128)}, u32[]{:S(2)}) copy-start(s32[512,1]{0,1:T(1,128)} %param.7) | copy-start | bytes 6148
  71.6 29.8 %copy-start.2 = (s32[512]{0:T(512)S(1)}, s32[512]{0:T(512)}, u32[]{:S(2)}) copy-start(s32[512]{0:T(512)} %param.8) | copy-start | bytes 6148
  71.6 29.8 %copy-start.3 = (s32[512]{0:T(512)S(1)}, s32[512]{0:T(512)}, u32[]{:S(2)}) copy-start(s32[512]{0:T(512)} %param.9) | copy-start | bytes 6148
  78.9 21.2 %all-to-all-start.3 = ((f32[64,1,128]{2,1,0:T(1,128)}), f32[64,1,128]{2,1,0:T(1,128)S(1)}, u32[]{:S(2)}, u32[]{:S(2)}) async-start(f32[64,1,128]{2,1,0:T(1,128)} %bitcast.16), calls=%async_computation.3 | async-start | bytes 65536 | tf_op jit(solution)/shard_map/all_to_all | solution.py:421
  101.7 0.6 copy-start.4

commit v5 on v4

--- a/solution.py
+++ b/solution.py
@@ -18,7 +18,6 @@
 TILE = 256
 TILES = 6
 PACKED = TILE * TILES
-ROOM = PACKED
 SPILL = 128
 GROUPS = [[g * 8 + b for g in range(core, 16, 2) for b in range(8)] for core in range(2)]
 COLS = (((1,), (1,)), ((), ()))
@@ -116,19 +115,9 @@
     return dot(pick, taken[rows, :]), dot(pick, fields, COLS)
 
 
-def load_chunks(source, taken, copied):
-    copies = []
-    for at in range(taken.shape[0] // CHUNK):
-        rows = pl.ds(at * CHUNK, CHUNK)
-        copies.append(pltpu.make_async_copy(source.at[rows, :], taken.at[rows, :], copied.at[at]))
-        copies[-1].start()
-    return copies
-
-
-def read_kernel(source, spill, spots, fields, info, taken, pile, ends, strange, copied):
+def read_kernel(taken, spill, spots, fields, info, pile, ends, strange):
     chunks = taken.shape[0] // CHUNK
     width = taken.shape[1]
-    copies = load_chunks(source, taken, copied)
     upto = hot(iota((CHUNK, CHUNK), 0) <= iota((CHUNK, CHUNK), 1))
     place = iota((EXTRA, CHUNK), 1)
     sender = jnp.zeros(place.shape, I32)
@@ -137,8 +126,6 @@
     spread = hot(place - sender * BLOCK == iota((EXTRA, CHUNK), 0))
     mine = (iota((64, CHUNK), 0) & 7) == sender[:64, :]
     spots[...] = jnp.full(spots.shape, -1, I32)
-    for copy in copies:
-        copy.wait()
     for at in range(CHIPS):
         last = at * BLOCK + SEATS
         top = (last // 16) * 16
@@ -192,46 +179,32 @@
     spill[...] = pile[...].astype(BF16)
 
 
-def pack_kernel(info, source, spots, fields, packed, taken, room, copied, placed):
-    chunks = taken.shape[0] // CHUNK
+def pack_kernel(info, taken, spots, fields, packed):
     width = taken.shape[1]
-    copies = load_chunks(source, taken, copied)
     tiles = info[16]
-    room[0:16, :] = jnp.zeros((16, room.shape[1]), BF16)
+    packed[0:16, :] = jnp.zeros((16, packed.shape[1]), BF16)
     first = jnp.int32(0)
-    done = jnp.int32(0)
-
-    def put(at):
-        rows = pl.ds(pl.multiple_of(at * TILE, TILE), TILE)
-        return pltpu.make_async_copy(room.at[rows, :], packed.at[rows, :], placed.at[at])
-
-    for at in range(chunks):
-        first = pl.multiple_of(jnp.minimum(info[at], ROOM - WINDOW), 16)
+    for at in range(taken.shape[0] // CHUNK):
+        first = pl.multiple_of(jnp.minimum(info[at], PACKED - WINDOW), 16)
         spot = spots[at : at + 1, 0:CHUNK] - first
-        copies[at].wait()
         rows_in, side = gather(spot, WINDOW, taken, pl.ds(at * CHUNK, CHUNK), fields[at])
         here = pl.ds(first, 16)
         after = pl.ds(pl.multiple_of(first + 16, 16), WINDOW - 16)
         for span, value in ((pl.ds(0, width), rows_in), (pl.ds(width, EXTRA), side)):
-            room[here, span] = (room[here, span].astype(F32) + value[:16]).astype(BF16)
-            room[after, span] = value[16:].astype(BF16)
-        if at + 1 < chunks:
-            filled = info[at + 1] // TILE
-            pl.when(filled > done)(put(done).start)
-            done = filled
-
-    def clear(at, carry):
-        room[pl.ds(pl.multiple_of(at * 16, 16), 16), :] = jnp.zeros((16, room.shape[1]), BF16)
+            packed[here, span] = (packed[here, span].astype(F32) + value[:16]).astype(BF16)
+            packed[after, span] = value[16:].astype(BF16)
+    clear(packed, (first + WINDOW) // 16, tiles * (TILE // 16))
+
+
+def clear(rows, low, high):
+    def step(at, carry):
+        rows[pl.ds(pl.multiple_of(at * 16, 16), 16), :] = jnp.zeros((16, rows.shape[1]), BF16)
         return carry
 
-    lax.fori_loop((first + WINDOW) // 16, tiles * (TILE // 16), clear, 0)
-    for at in range(TILES):
-        pl.when((at >= done) & (at < tiles))(put(at).start)
-    for at in range(TILES):
-        pl.when(at < tiles)(put(at).wait)
-
-
-def append_kernel(info, near, packed_in, packed, info_out, window, blank, sems):
+    lax.fori_loop(low, high, step, 0)
+
+
+def append_kernel(info, near, packed_in, packed, info_out):
     for at in range(20):
         info_out[at] = info[at]
     total, tiles = info[18], info[16]
@@ -247,37 +220,15 @@
     def _():
         more = (total + count + TILE - 1) // TILE
         info_out[16] = more
-        begin = pl.multiple_of(first, 16)
-        head = pltpu.make_async_copy(
-            packed.at[pl.ds(begin, 16), :], window.at[pl.ds(0, 16), :], sems.at[0]
-        )
-        head.start()
-
-        @pl.when(more > tiles)
-        def _():
-            blank[...] = jnp.zeros(blank.shape, BF16)
-
+        clear(packed, tiles * (TILE // 16), more * (TILE // 16))
         shift = iota((SPILL + 16, SPILL), 0) - iota((SPILL + 16, SPILL), 1)
         moved = dot(hot(shift == total - first), near[...])
-        head.wait()
         keep = iota((16, packed.shape[1]), 0) < total - first
-        window[0:16, :] = jnp.where(
-            keep, window[0:16, :].astype(F32), moved[:16]
-        ).astype(BF16)
-        window[16:, :] = moved[16:].astype(BF16)
-
-        @pl.when(more > tiles)
-        def _():
-            at = pl.multiple_of(tiles * TILE, TILE)
-            clear = pltpu.make_async_copy(blank, packed.at[pl.ds(at, TILE), :], sems.at[1])
-            clear.start()
-            clear.wait()
-
-        put = pltpu.make_async_copy(
-            window, packed.at[pl.ds(begin, SPILL + 16), :], sems.at[2]
-        )
-        put.start()
-        put.wait()
+        here = pl.ds(pl.multiple_of(first, 16), 16)
+        after = pl.ds(pl.multiple_of(first + 16, 16), SPILL)
+        held = packed[here, :].astype(F32)
+        packed[here, :] = jnp.where(keep, held, moved[:16]).astype(BF16)
+        packed[after, :] = moved[16:].astype(BF16)
 
 
 def score(queries, query_tiles, keys, key_tiles, best, marks, bounds):
@@ -316,39 +267,17 @@
         pl.when(key_tiles == tiles)(functools.partial(against, tiles * TILE))
 
 
-def fetch(source, target, tiles, sems):
-    for at in range(TILES):
-        rows = pl.ds(at * TILE, TILE)
-        copy = pltpu.make_async_copy(source.at[rows, :], target.at[rows, :], sems.at[at])
-        pl.when(at < tiles)(copy.start)
-
-
-def fetched(source, target, tiles, sems):
-    for at in range(TILES):
-        rows = pl.ds(at * TILE, TILE)
-        copy = pltpu.make_async_copy(source.at[rows, :], target.at[rows, :], sems.at[at])
-        pl.when(at < tiles)(copy.wait)
-
-
-def own_kernel(info, packed, best, mine, marks, bounds, sems):
-    fetch(packed, mine, info[16], sems)
+def own_kernel(info, packed, best, marks, bounds):
     best[...] = jnp.full(best.shape, -1.0, F32)
-    fetched(packed, mine, info[16], sems)
-    score(mine, info[16], mine, info[16], best, marks, bounds)
+    score(packed, info[16], packed, info[16], best, marks, bounds)
 
 
 def other_kernel(
-    info, other_info, packed, other, near, best_in, spots, back,
-    mine, theirs, best, split, marks, bounds, sems, other_sems,
+    info, other_info, mine, theirs, near, best_in, spots, back, best, split, marks, bounds
 ):
-    tiles, other_tiles = info[16], other_info[16]
-    fetch(packed, mine, tiles, sems)
-    fetch(other, theirs, other_tiles, other_sems)
     best[:, :PACKED] = best_in[...]
     best[:, PACKED:] = jnp.full((1, best.shape[1] - PACKED), -1.0, F32)
-    fetched(packed, mine, tiles, sems)
-    fetched(other, theirs, other_tiles, other_sems)
-    score(mine, tiles, theirs, other_tiles, best, marks, bounds)
+    score(mine, info[16], theirs, other_info[16], best, marks, bounds)
     flag = jnp.maximum(info[17], other_info[17]).astype(F32)
     reach = 384
     row = iota((16, best.shape[1]), 0)
@@ -408,9 +337,13 @@
 
 
 SCALARS = pl.BlockSpec(memory_space=pltpu.SMEM)
-PLACED = pl.BlockSpec(memory_space=pl.ANY)
+HELD = pl.BlockSpec(memory_space=pltpu.VMEM)
 
 LESS = pltpu.CompilerParams(vmem_limit_bytes=28 * 1024 * 1024)
+
+
+def held(x):
+    return pltpu.with_memory_space_constraint(x, pltpu.VMEM)
 
 
 def array(shape, dtype):
@@ -446,100 +379,72 @@
     taken = exchange(sent.reshape(CHIPS, BLOCK, width)).reshape(lines, width)
     spill, spots, fields, info = pl.pallas_call(
         read_kernel,
-        in_specs=[PLACED],
-        out_specs=[
-            whole((SPILL, full)),
-            whole((chunks, 2 * EXTRA)),
-            whole((chunks, EXTRA, CHUNK)),
-            SCALARS,
-        ],
+        in_specs=[HELD],
+        out_specs=[HELD, HELD, HELD, SCALARS],
         out_shape=[
-            array((SPILL, full), BF16),
-            array((chunks, 2 * EXTRA), I32),
-            array((chunks, EXTRA, CHUNK), BF16),
+            pltpu.VMEM((SPILL, full), BF16),
+            pltpu.VMEM((chunks, 2 * EXTRA), I32),
+            pltpu.VMEM((chunks, EXTRA, CHUNK), BF16),
             array((32,), I32),
         ],
         scratch_shapes=[
-            pltpu.VMEM((lines, width), BF16),
             pltpu.VMEM((SPILL, full), F32),
             pltpu.VMEM((CHIPS, width), F32),
             pltpu.VMEM((chunks, CHUNK), I32),
-            pltpu.SemaphoreType.DMA((chunks,)),
         ],
         compiler_params=LESS,
         name="read",
-    )(taken)
+    )(held(taken))
     near = lax.ppermute(spill, BOTH, [(i, i ^ 1) for i in range(2 * CHIPS)])
     packed = pl.pallas_call(
         pack_kernel,
-        in_specs=[SCALARS, PLACED, whole((chunks, 2 * EXTRA)), whole((chunks, EXTRA, CHUNK))],
-        out_specs=PLACED,
-        out_shape=array((PACKED, full), BF16),
-        scratch_shapes=[
-            pltpu.VMEM((lines, width), BF16),
-            pltpu.VMEM((ROOM, full), BF16),
-            pltpu.SemaphoreType.DMA((chunks,)),
-            pltpu.SemaphoreType.DMA((TILES,)),
-        ],
+        in_specs=[SCALARS, HELD, HELD, HELD],
+        out_specs=HELD,
+        out_shape=pltpu.VMEM((PACKED, full), BF16),
         compiler_params=LESS,
         cost_estimate=pl.CostEstimate(
             flops=2 * lines * WINDOW * full, bytes_accessed=4 * lines * full, transcendentals=0
         ),
         name="pack",
-    )(info, taken, spots, fields)
+    )(info, held(taken), held(spots), held(fields))
     packed, info = pl.pallas_call(
         append_kernel,
-        in_specs=[SCALARS, whole((SPILL, full)), PLACED],
-        out_specs=[PLACED, SCALARS],
-        out_shape=[array((PACKED, full), BF16), array((32,), I32)],
-        scratch_shapes=[
-            pltpu.VMEM((SPILL + 16, full), BF16),
-            pltpu.VMEM((TILE, full), BF16),
-            pltpu.SemaphoreType.DMA((3,)),
-        ],
+        in_specs=[SCALARS, HELD, HELD],
+        out_specs=[HELD, SCALARS],
+        out_shape=[pltpu.VMEM((PACKED, full), BF16), array((32,), I32)],
         input_output_aliases={2: 0},
         compiler_params=LESS,
         name="append",
-    )(info, near, packed)
+    )(info, held(near), held(packed))
     swap = [(i, i ^ 1) for i in range(16)]
     other_info = lax.ppermute(info, "grp", swap)
     other = lax.ppermute(packed, "grp", swap)
     best = pl.pallas_call(
         own_kernel,
-        in_specs=[SCALARS, PLACED],
-        out_specs=whole((1, PACKED)),
-        out_shape=array((1, PACKED), F32),
-        scratch_shapes=[
-            pltpu.VMEM((PACKED, full), BF16),
-            pltpu.VMEM((PACKED, EXTRA), I32),
-            pltpu.VMEM((8, PACKED), I32),
-            pltpu.SemaphoreType.DMA((TILES,)),
-        ],
+        in_specs=[SCALARS, HELD],
+        out_specs=HELD,
+        out_shape=pltpu.VMEM((1, PACKED), F32),
+        scratch_shapes=[pltpu.VMEM((PACKED, EXTRA), I32), pltpu.VMEM((8, PACKED), I32)],
         compiler_params=LESS,
         cost_estimate=pl.CostEstimate(
             flops=2 * 1024 * 1024 * width, bytes_accessed=2 * PACKED * full, transcendentals=0
         ),
         name="own",
-    )(info, packed)
+    )(info, held(packed))
     back = pl.pallas_call(
         other_kernel,
-        in_specs=[SCALARS, SCALARS, PLACED, PLACED]
-        + [whole((SPILL, full)), whole((1, PACKED)), whole((chunks, 2 * EXTRA))],
-        out_specs=whole((CHIPS, EXTRA)),
-        out_shape=array((CHIPS, EXTRA), F32),
+        in_specs=[SCALARS, SCALARS] + [HELD] * 5,
+        out_specs=HELD,
+        out_shape=pltpu.VMEM((CHIPS, EXTRA), F32),
         scratch_shapes=[
-            pltpu.VMEM((PACKED, full), BF16),
-            pltpu.VMEM((PACKED, full), BF16),
             pltpu.VMEM((1, PACKED + 2 * TILE), F32),
             pltpu.VMEM((16, PACKED + 2 * TILE), BF16),
             pltpu.VMEM((PACKED, EXTRA), I32),
             pltpu.VMEM((8, PACKED), I32),
-            pltpu.SemaphoreType.DMA((TILES,)),
-            pltpu.SemaphoreType.DMA((TILES,)),
         ],
         compiler_params=LESS,
         name="other",
-    )(info, other_info, packed, other, near, best, spots)
+    )(info, other_info, held(packed), held(other), held(near), held(best), held(spots))
     home = exchange(back)
     highest, flag = pl.pallas_call(
         home_kernel,

time: 103 us -> 102 us (level); the launches traced: 102 us -> 103 us
  Pallas kernels: 21 us -> 15.2 us
  starting transfers between devices: 12.8 us -> 16.1 us
  waiting for transfers between devices: 14.2 us -> 17.5 us
    pallas_call x5, Pallas kernels: 16.1 us -> 10.3 us  [the longest x1 3.44 us: direct(): pl.pallas_call(other_kernel, in_specs=[SCALARS, SCALARS] + [HELD] * 5, ou...]
    all_to_all x1, starting transfers between devices: 11.6 us -> 14.8 us  [exchange(): lax.all_to_all(x, BOTH, split_axis=0, concat_axis=0, tiled=True, axis_ind...]
    ppermute x1, waiting for transfers between devices: 1.6 us -> 4.62 us  [direct(): near = lax.ppermute(spill, BOTH, [(i, i ^ 1) for i in range(2 * CHIPS)])]
  transfers between devices with their start and end apart: 4 -> 4, of which waited for: 3 -> 3; matrix products, arithmetic and copies ran while one was open for 0% -> 0% of each run, Pallas kernels for 8% -> 4%
where the time goes in v5:
time: 102 us; the launch traced here: 103 us
  blocking collectives  52.7 us (52%)
  waiting for transfers between devices  17.5 us (17%)
  starting transfers between devices  16.1 us (16%)
  Pallas kernels  15.2 us (15%)
    all_to_all x1, blocking collectives, exchange(): lax.all_to_all(x, BOTH, split_axis=0, concat_axis=0, tiled=True, axis_ind...  52.7 us
    all_to_all x1, starting transfers between devices, exchange(): lax.all_to_all(x, BOTH, split_axis=0, concat_axis=0, tiled=True, axis_ind...  14.8 us
    all_to_all x1, waiting for transfers between devices, exchange(): lax.all_to_all(x, BOTH, split_axis=0, concat_axis=0, tiled=True, axis_ind...  9.55 us
    ppermute x1, waiting for transfers between devices, direct(): near = lax.ppermute(spill, BOTH, [(i, i ^ 1) for i in range(2 * CHIPS)])  4.62 us
    pallas_call x1, Pallas kernels, direct(): pl.pallas_call(send_kernel, grid=(chunks // 2,), in_specs=[SCALARS, whole...  4.15 us
    pallas_call x1, Pallas kernels, direct(): pl.pallas_call(other_kernel, in_specs=[SCALARS, SCALARS] + [HELD] * 5, ou...  3.44 us
    ppermute x1, waiting for transfers between devices, direct(): other_info = lax.ppermute(info, 'grp', swap)  3.35 us
    pallas_call x1, Pallas kernels, direct(): pl.pallas_call(own_kernel, in_specs=[SCALARS, HELD], out_specs=HELD, out_...  2.31 us
  transfers between devices with their start and end apart: 4, of which 3 were waited for; matrix products, arithmetic and copies ran while one was open for 0% of the time, Pallas kernels for 4%

profile of v5, /device:TPU:0, one launch (start us, length us, event | category | flops | bytes accessed | tf_op | source)
XLA Modules:
  0.0 102.8 jit_solution(10353204357621912926)
XLA Ops:
  0.0 4.2 %send.1 = (bf16[1536,1024]{1,0:T(8,128)(2,1)S(1)}, s32[8,512]{1,0:T(8,128)S(1)}) custom-call(s32[1]{0:T(128)} %bitcast.9.me, bf16[512,1024]{1,0:T(8,128)(2,1)} %embed.1, s32[1,512]{1,0:T(1,128)} %bitcast.56, s32[1,512]{1,0:T(1,128)} %bitcast.59, s32[1,512]{1,0:T(1,128)} %bitcast.60), custom_call_target="tpu_custom_call" | custom-call | tf_op jit(solution)/shard_map/send/pallas_call | solution.py:365
  4.2 52.7 %all_to_all.28 = bf16[64,24,1024]{2,1,0:T(8,128)(2,1)S(1)} all-to-all(bf16[64,24,1024]{2,1,0:T(8,128)(2,1)S(1)} %bitcast.53), channel_id=1, replica_groups={{0,1,2,3,4,5,6,7,16,17,18,19,20,21,22,23,32,33,34,35,36,37,38,39,48,49,..., dimensions={0} | all-to-all | bytes 6291456 | tf_op jit(solution)/shard_map/all_to_all | solution.py:354
  56.8 1.2 %read.1 = (bf16[128,1152]{1,0:T(8,128)(2,1)S(1)}, s32[8,256]{1,0:T(8,128)S(1)}, bf16[8,128,192]{2,1,0:T(8,128)(2,1)S(1)}, s32[32]{0:T(128)S(1)}) custom-call(bf16[1536,1024]{1,0:T(8,128)(2,1)S(1)} %bitcast.51), custom_call_target="tpu_custom_call" | custom-call | tf_op jit(solution)/shard_map/read/pallas_call | solution.py:380
  58.0 0.6 collective-permute-start.7
  58.7 2.0 %pack.1.packed_in = bf16[1536,1152]{1,0:T(8,128)(2,1)S(1)} custom-call(s32[32]{0:T(128)S(1)} %get-tuple-element.34.info, bf16[1536,1024]{1,0:T(8,128)(2,1)S(1)} %bitcast.52, s32[8,256]{1,0:T(8,128)S(1)} %get-tuple-element.36.spots, bf16[8,128,192]{2,1,0:T(8,128)(2,1)S(1)} %get-tuple-element.37.fields), custom_call_target="tpu_custom_call" | custom-call | flops 736100352 | bytes 7077888 | tf_op jit(solution)/shard_map/pack/pallas_call | solution.py:399
  60.7 4.6 %collective-permute-done.7.near = bf16[128,1152]{1,0:T(8,128)(2,1)S(1)} collective-permute-done((bf16[128,1152]{1,0:T(8,128)(2,1)S(1)}, bf16[128,1152]{1,0:T(8,128)(2,1)S(1)}, u32[]{:S(2)}, u32[]{:S(2)}) %collective-permute-start.7) | collective-permute-done | bytes 294944 | tf_op jit(solution)/shard_map/ppermute | solution.py:398
  65.3 1.3 %append.1 = (bf16[1536,1152]{1,0:T(8,128)(2,1)S(1)}, s32[32]{0:T(128)S(1)}) custom-call(s32[32]{0:T(128)S(1)} %get-tuple-element.34.info, bf16[128,1152]{1,0:T(8,128)(2,1)S(1)} %collective-permute-done.7.near, bf16[1536,1152]{1,0:T(8,128)(2,1)S(1)} %pack.1.packed_in), custom_call_target="tpu_custom_call", output_to_operand_aliasing={{0}: (2, {})} | custom-call | tf_op jit(solution)/shard_map/append/pallas_call | solution.py:410
  66.7 0.1 collective-permute-start.9
  66.8 0.5 collective-permute-start.8
  67.3 2.3 %own.1.best_in = f32[1,1536]{1,0:T(1,128)S(1)} custom-call(s32[32]{0:T(128)S(1)} %get-tuple-element.38.info, bf16[1536,1152]{1,0:T(8,128)(2,1)S(1)} %get-tuple-element.39.packed.mine), custom_call_target="tpu_custom_call" | custom-call | flops 2147483648 | bytes 3538944 | tf_op jit(solution)/shard_map/own/pallas_call | solution.py:422
  69.6 0.0 copy-start
  69.6 0.0 copy-start.1
  69.6 0.0 copy-start.2
  69.6 0.0 copy-start.3
  69.7 3.3 %collective-permute-done.8.other_info = s32[32]{0:T(128)S(1)} collective-permute-done((s32[32]{0:T(128)S(1)}, s32[32]{0:T(128)S(1)}, u32[]{:S(2)}, u32[]{:S(2)}) %collective-permute-start.8) | collective-permute-done | bytes 160 | tf_op jit(solution)/shard_map/ppermute | solution.py:420
  73.0 0.0 collective-permute-done.9.theirs
  73.0 3.4 %other.1 = f32[64,128]{1,0:T(8,128)} custom-call(s32[32]{0:T(128)S(1)} %get-tuple-element.38.info, s32[32]{0:T(128)S(1)} %collective-permute-done.8.other_info, bf16[1536,1152]{1,0:T(8,128)(2,1)S(1)} %get-tuple-element.39.packed.mine, bf16[1536,1152]{1,0:T(8,128)(2,1)S(1)} %collective-permute-done.9.theirs, ...), custom_call_target="tpu_custom_call" | custom-call | tf_op jit(solution)/shard_map/other/pallas_call | solution.py:434
  76.4 14.8 %all-to-all-start.3 = ((f32[64,1,128]{2,1,0:T(1,128)}), f32[64,1,128]{2,1,0:T(1,128)S(1)}, u32[]{:S(2)}, u32[]{:S(2)}) async-start(f32[64,1,128]{2,1,0:T(1,128)} %bitcast.16), calls=%async_computation.3 | async-start | bytes 65536 | tf_op jit(solution)/shard_map/all_to_all | solution.py:354
  91.3 9.6 %all-to-all-done.3 = f32[64,1,128]{2,1,0:T(1,128)S(1)} async-done(((f32[64,1,128]{2,1,0:T(1,128)}), f32[64,1,128]{2,1,0:T(1,128)S(1)}, u32[]{:S(2)}, u32[]{:S(2)}) %all-to-all-start.3) | async-done | bytes 32800 | tf_op jit(solution)/shard_map/all_to_all | solution.py:354
  100.8 0.7 home.1
  102.2 0.0 copy-done
  102.2 0.0 copy-done.1
  102.2 0.0 copy-done.2
  102.2 0.0 copy-done.3
  102.2 0.0 copy-start.4
  102.3 0.6 copy-done.4
  (1 shorter events, 0.0 us)
Async XLA Ops:
  58.0 7.3 %collective-permute-start.7 = (bf16[128,1152]{1,0:T(8,128)(2,1)S(1)}, bf16[128,1152]{1,0:T(8,128)(2,1)S(1)}, u32[]{:S(2)}, u32[]{:S(2)}) collective-permute-start(bf16[128,1152]{1,0:T(8,128)(2,1)S(1)} %get-tuple-element.35), channel_id=1, source_target_pairs={{0,1},{1,0},{2,3},{3,2},{4,5},{5,4},{6,7},{7,6},{8,9},{9,8},{10,11... | collective-permute-start | bytes 884744 | tf_op jit(solution)/shard_map/ppermute | solution.py:398
  66.7 6.3 %collective-permute-start.9 = (bf16[1536,1152]{1,0:T(8,128)(2,1)S(1)}, bf16[1536,1152]{1,0:T(8,128)(2,1)S(1)}, u32[]{:S(2)}, u32[]{:S(2)}) collective-permute-start(bf16[1536,1152]{1,0:T(8,128)(2,1)S(1)} %get-tuple-element.39.packed.mine), channel_id=1, source_target_pairs={{0,8},{8,0},{16,24},{24,16},{32,40},{40,32},{48,56},{56,48},{64,72... | collective-permute-start | bytes 10616840 | tf_op jit(solution)/shard_map/ppermute | solution.py:421
  66.8 6.2 %collective-permute-start.8 = (s32[32]{0:T(128)S(1)}, s32[32]{0:T(128)S(1)}, u32[]{:S(2)}, u32[]{:S(2)}) collective-permute-start(s32[32]{0:T(128)S(1)} %get-tuple-element.38.info), channel_id=1, source_target_pairs={{0,8},{8,0},{16,24},{24,16},{32,40},{40,32},{48,56},{56,48},{64,72... | collective-permute-start | bytes 392 | tf_op jit(solution)/shard_map/ppermute | solution.py:420
  69.6 32.6 %copy-start = (bf16[512,1024]{1,0:T(8,128)(2,1)S(1)}, bf16[512,1024]{1,0:T(8,128)(2,1)}, u32[]{:S(2)}) copy-start(bf16[512,1024]{1,0:T(8,128)(2,1)} %embed.1) | copy-start | bytes 3145732
  69.6 32.6 %copy-start.1 = (s32[512,1]{0,1:T(1,128)S(1)}, s32[512,1]{0,1:T(1,128)}, u32[]{:S(2)}) copy-start(s32[512,1]{0,1:T(1,128)} %param.7) | copy-start | bytes 6148
  69.6 32.6 %copy-start.2 = (s32[512]{0:T(512)S(1)}, s32[512]{0:T(512)}, u32[]{:S(2)}) copy-start(s32[512]{0:T(512)} %param.8) | copy-start | bytes 6148
  69.6 32.6 %copy-start.3 = (s32[512]{0:T(512)S(1)}, s32[512]{0:T(512)}, u32[]{:S(2)}) copy-start(s32[512]{0:T(512)} %param.9) | copy-start | bytes 6148
  76.4 24.4 %all-to-all-start.3 = ((f32[64,1,128]{2,1,0:T(1,128)}), f32[64,1,128]{2,1,0:T(1,128)S(1)}, u32[]{:S(2)}, u32[]{:S(2)}) async-start(f32[64,1,128]{2,1,0:T(1,128)} %bitcast.16), calls=%async_computation.3 | async-start | bytes 65536 | tf_op jit(solution)/shard_map/all_to_all | solution.py:354
  102.2 0.6 copy-start.4

commit v6 on v5

--- a/solution.py
+++ b/solution.py
@@ -50,7 +50,14 @@
     return dot(hot(iota((16, EXTRA), 0) == iota((16, EXTRA), 1)), extra, COLS)
 
 
-def send_kernel(me, embed, owner, local, rank, out, place, unit, slot, ends):
+def chip_of(group, number, attempt):
+    if attempt == 0:
+        return (number >> 1) ^ (group * 4)
+    turned = ((number >> 3) | (number << 4)) & (CHIPS - 1)
+    return turned ^ (((group * 5 + 2) & 15) * 4)
+
+
+def send_kernel(attempt, me, embed, owner, local, rank, out, place, unit, slot, ends):
     rows, width = embed.shape
     step = pl.program_id(0)
     block = out.shape[0]
@@ -61,7 +68,7 @@
         scale = lax.rsqrt(jnp.sum(wide * wide, 1, keepdims=True) + EPS)
         unit[...] = (wide * scale).astype(BF16)
         group, number, order = owner[...], local[...], rank[...]
-        chip = (number & (CHIPS - 1)) ^ (group * 4)
+        chip = chip_of(group, number, attempt)
         own = iota((CHIPS, rows), 0) == chip
         near = iota((CHIPS, rows), 0) == (chip ^ 1)
         before = hot(iota((rows, rows), 0) < iota((rows, rows), 1))
@@ -209,8 +216,8 @@
         info_out[at] = info[at]
     total, tiles = info[18], info[16]
     count = jnp.sum(near[:, packed.shape[1] - EXTRA :].astype(F32)[:, 4:5]).astype(I32)
-    first = (total >> 4) << 4
-    fits = (total + count <= PACKED) & (first + SPILL + 16 <= PACKED)
+    begin = jnp.minimum((total >> 4) << 4, PACKED - SPILL - 16)
+    fits = total + count <= PACKED
 
     @pl.when((count > 0) & jnp.logical_not(fits))
     def _():
@@ -222,13 +229,10 @@
         info_out[16] = more
         clear(packed, tiles * (TILE // 16), more * (TILE // 16))
         shift = iota((SPILL + 16, SPILL), 0) - iota((SPILL + 16, SPILL), 1)
-        moved = dot(hot(shift == total - first), near[...])
-        keep = iota((16, packed.shape[1]), 0) < total - first
-        here = pl.ds(pl.multiple_of(first, 16), 16)
-        after = pl.ds(pl.multiple_of(first + 16, 16), SPILL)
-        held = packed[here, :].astype(F32)
-        packed[here, :] = jnp.where(keep, held, moved[:16]).astype(BF16)
-        packed[after, :] = moved[16:].astype(BF16)
+        moved = dot(hot(shift == total - begin), near[...])
+        keep = iota(moved.shape, 0) < total - begin
+        here = pl.ds(pl.multiple_of(begin, 16), SPILL + 16)
+        packed[here, :] = jnp.where(keep, packed[here, :].astype(F32), moved).astype(BF16)
 
 
 def score(queries, query_tiles, keys, key_tiles, best, marks, bounds):
@@ -356,14 +360,14 @@
     )
 
 
-def direct(embed, owner, local_id, rank):
+def direct(attempt, embed, owner, local_id, rank):
     rows, width = embed.shape
     full = width + EXTRA
     lines = CHIPS * BLOCK
     chunks = lines // CHUNK
     me = ((lax.axis_index("grp") >> 1) * 8 + lax.axis_index("blk")).astype(I32).reshape(1)
     sent, place = pl.pallas_call(
-        send_kernel,
+        functools.partial(send_kernel, attempt),
         grid=(chunks // 2,),
         in_specs=[SCALARS, whole((rows, width))] + [whole((1, rows))] * 3,
         out_specs=[pl.BlockSpec((2 * CHUNK, width), lambda i: (i, 0)), whole((8, rows))],
@@ -499,11 +503,14 @@
     return home.reshape(width)[slot_index]
 
 
-def per_device(embed, owner, local_id, rank):
-    highest, flag = direct(embed, owner, local_id, rank)
-    return lax.cond(
-        flag > 0, lambda: by_group(embed, owner, local_id, rank), lambda: highest
-    )
+def per_device(*arrays):
+    highest, flag = direct(0, *arrays)
+
+    def again():
+        second, still = direct(1, *arrays)
+        return lax.cond(still > 0, lambda: by_group(*arrays), lambda: second)
+
+    return lax.cond(flag > 0, again, lambda: highest)
 
 
 def solution(mesh):

time: 102 us -> 99.5 us (0.975); the launches traced: 103 us -> 99.3 us
  starting transfers between devices: 16.1 us -> 10.1 us
  Pallas kernels: 15.2 us -> 17.3 us
    all_to_all x1, starting transfers between devices: 14.8 us -> 9.39 us  [exchange(): lax.all_to_all(x, BOTH, split_axis=0, concat_axis=0, tiled=True, axis_ind...]
    pallas_call x1, Pallas kernels: 1.2 us -> 3.17 us  [direct(): pl.pallas_call(read_kernel, in_specs=[HELD], out_specs=[HELD, HELD, HELD,...]
where the time goes in v6:
time: 99.5 us; the launch traced here: 99.3 us
  blocking collectives  52.7 us (53%)
  waiting for transfers between devices  18.1 us (18%)
  Pallas kernels  17.3 us (17%)
  starting transfers between devices  10.1 us (10%)
    all_to_all x1, blocking collectives, exchange(): lax.all_to_all(x, BOTH, split_axis=0, concat_axis=0, tiled=True, axis_ind...  52.7 us
    all_to_all x1, waiting for transfers between devices, exchange(): lax.all_to_all(x, BOTH, split_axis=0, concat_axis=0, tiled=True, axis_ind...  9.55 us
    all_to_all x1, starting transfers between devices, exchange(): lax.all_to_all(x, BOTH, split_axis=0, concat_axis=0, tiled=True, axis_ind...  9.39 us
    ppermute x1, waiting for transfers between devices, direct(): near = lax.ppermute(spill, BOTH, [(i, i ^ 1) for i in range(2 * CHIPS)])  5.17 us
    pallas_call x1, Pallas kernels, direct(): pl.pallas_call(functools.partial(send_kernel, attempt), grid=(chunks // 2...  4.15 us
    pallas_call x1, Pallas kernels, direct(): pl.pallas_call(other_kernel, in_specs=[SCALARS, SCALARS] + [HELD] * 5, ou...  3.43 us
    ppermute x1, waiting for transfers between devices, direct(): other_info = lax.ppermute(info, 'grp', swap)  3.36 us
    pallas_call x1, Pallas kernels, direct(): pl.pallas_call(read_kernel, in_specs=[HELD], out_specs=[HELD, HELD, HELD,...  3.17 us
  transfers between devices with their start and end apart: 4, of which 3 were waited for; matrix products, arithmetic and copies ran while one was open for 0% of the time, Pallas kernels for 4%

profile of v6, /device:TPU:0, one launch (start us, length us, event | category | flops | bytes accessed | tf_op | source)
XLA Modules:
  0.0 99.3 jit_solution(11036807279136377059)
XLA Ops:
  0.0 4.2 %send.3 = (bf16[1536,1024]{1,0:T(8,128)(2,1)S(1)}, s32[8,512]{1,0:T(8,128)S(1)}) custom-call(s32[1]{0:T(128)} %bitcast.21.me, bf16[512,1024]{1,0:T(8,128)(2,1)} %embed.1, s32[1,512]{1,0:T(1,128)} %bitcast.72, s32[1,512]{1,0:T(1,128)} %bitcast.76, s32[1,512]{1,0:T(1,128)} %bitcast.78), custom_call_target="tpu_custom_call" | custom-call | tf_op jit(solution)/shard_map/send/pallas_call | solution.py:369
  4.2 52.7 %all_to_all.41 = bf16[64,24,1024]{2,1,0:T(8,128)(2,1)S(1)} all-to-all(bf16[64,24,1024]{2,1,0:T(8,128)(2,1)S(1)} %bitcast.67), channel_id=1, replica_groups={{0,1,2,3,4,5,6,7,16,17,18,19,20,21,22,23,32,33,34,35,36,37,38,39,48,49,..., dimensions={0} | all-to-all | bytes 6291456 | tf_op jit(solution)/shard_map/all_to_all | solution.py:358
  56.8 3.2 %read.3 = (bf16[128,1152]{1,0:T(8,128)(2,1)S(1)}, s32[8,256]{1,0:T(8,128)S(1)}, bf16[8,128,192]{2,1,0:T(8,128)(2,1)S(1)}, s32[32]{0:T(128)S(1)}) custom-call(bf16[1536,1024]{1,0:T(8,128)(2,1)S(1)} %bitcast.63), custom_call_target="tpu_custom_call" | custom-call | tf_op jit(solution)/shard_map/read/pallas_call | solution.py:384
  60.0 0.1 collective-permute-start.10
  60.1 2.0 %pack.3.packed_in = bf16[1536,1152]{1,0:T(8,128)(2,1)S(1)} custom-call(s32[32]{0:T(128)S(1)} %get-tuple-element.62.info, bf16[1536,1024]{1,0:T(8,128)(2,1)S(1)} %bitcast.64, s32[8,256]{1,0:T(8,128)S(1)} %get-tuple-element.64.spots, bf16[8,128,192]{2,1,0:T(8,128)(2,1)S(1)} %get-tuple-element.65.fields), custom_call_target="tpu_custom_call" | custom-call | flops 736100352 | bytes 7077888 | tf_op jit(solution)/shard_map/pack/pallas_call | solution.py:403
  62.1 5.2 %collective-permute-done.10.near = bf16[128,1152]{1,0:T(8,128)(2,1)S(1)} collective-permute-done((bf16[128,1152]{1,0:T(8,128)(2,1)S(1)}, bf16[128,1152]{1,0:T(8,128)(2,1)S(1)}, u32[]{:S(2)}, u32[]{:S(2)}) %collective-permute-start.10) | collective-permute-done | bytes 294944 | tf_op jit(solution)/shard_map/ppermute | solution.py:402
  67.3 1.3 %append.3 = (bf16[1536,1152]{1,0:T(8,128)(2,1)S(1)}, s32[32]{0:T(128)S(1)}) custom-call(s32[32]{0:T(128)S(1)} %get-tuple-element.62.info, bf16[128,1152]{1,0:T(8,128)(2,1)S(1)} %collective-permute-done.10.near, bf16[1536,1152]{1,0:T(8,128)(2,1)S(1)} %pack.3.packed_in), custom_call_target="tpu_custom_call", output_to_operand_aliasing={{0}: (2, {})} | custom-call | tf_op jit(solution)/shard_map/append/pallas_call | solution.py:414
  68.7 0.1 collective-permute-start.12
  68.8 0.5 collective-permute-start.11
  69.3 2.3 %own.3.best_in = f32[1,1536]{1,0:T(1,128)S(1)} custom-call(s32[32]{0:T(128)S(1)} %get-tuple-element.66.info, bf16[1536,1152]{1,0:T(8,128)(2,1)S(1)} %get-tuple-element.67.packed.mine), custom_call_target="tpu_custom_call" | custom-call | flops 2147483648 | bytes 3538944 | tf_op jit(solution)/shard_map/own/pallas_call | solution.py:426
  71.6 0.0 copy-start
  71.6 0.0 copy-start.1
  71.6 0.0 copy-start.2
  71.6 0.0 copy-start.3
  71.6 3.4 %collective-permute-done.11.other_info = s32[32]{0:T(128)S(1)} collective-permute-done((s32[32]{0:T(128)S(1)}, s32[32]{0:T(128)S(1)}, u32[]{:S(2)}, u32[]{:S(2)}) %collective-permute-start.11) | collective-permute-done | bytes 160 | tf_op jit(solution)/shard_map/ppermute | solution.py:424
  75.0 0.0 collective-permute-done.12.theirs
  75.0 3.4 %other.3 = f32[64,128]{1,0:T(8,128)} custom-call(s32[32]{0:T(128)S(1)} %get-tuple-element.66.info, s32[32]{0:T(128)S(1)} %collective-permute-done.11.other_info, bf16[1536,1152]{1,0:T(8,128)(2,1)S(1)} %get-tuple-element.67.packed.mine, bf16[1536,1152]{1,0:T(8,128)(2,1)S(1)} %collective-permute-done.12.theirs, ...), custom_call_target="tpu_custom_call" | custom-call | tf_op jit(solution)/shard_map/other/pallas_call | solution.py:438
  78.4 9.4 %all-to-all-start.5 = ((f32[64,1,128]{2,1,0:T(1,128)}), f32[64,1,128]{2,1,0:T(1,128)S(1)}, u32[]{:S(2)}, u32[]{:S(2)}) async-start(f32[64,1,128]{2,1,0:T(1,128)} %bitcast.28), calls=%async_computation.5 | async-start | bytes 65536 | tf_op jit(solution)/shard_map/all_to_all | solution.py:358
  87.8 9.6 %all-to-all-done.5 = f32[64,1,128]{2,1,0:T(1,128)S(1)} async-done(((f32[64,1,128]{2,1,0:T(1,128)}), f32[64,1,128]{2,1,0:T(1,128)S(1)}, u32[]{:S(2)}, u32[]{:S(2)}) %all-to-all-start.5) | async-done | bytes 32800 | tf_op jit(solution)/shard_map/all_to_all | solution.py:358
  97.3 0.9 home.3
  98.8 0.0 copy-done
  98.8 0.0 copy-done.1
  98.8 0.0 copy-done.2
  98.8 0.0 copy-done.3
  98.8 0.2 conditional.2
Async XLA Ops:
  60.0 7.3 %collective-permute-start.10 = (bf16[128,1152]{1,0:T(8,128)(2,1)S(1)}, bf16[128,1152]{1,0:T(8,128)(2,1)S(1)}, u32[]{:S(2)}, u32[]{:S(2)}) collective-permute-start(bf16[128,1152]{1,0:T(8,128)(2,1)S(1)} %get-tuple-element.63), channel_id=1, source_target_pairs={{0,1},{1,0},{2,3},{3,2},{4,5},{5,4},{6,7},{7,6},{8,9},{9,8},{10,11... | collective-permute-start | bytes 884744 | tf_op jit(solution)/shard_map/ppermute | solution.py:402
  68.7 6.3 %collective-permute-start.12 = (bf16[1536,1152]{1,0:T(8,128)(2,1)S(1)}, bf16[1536,1152]{1,0:T(8,128)(2,1)S(1)}, u32[]{:S(2)}, u32[]{:S(2)}) collective-permute-start(bf16[1536,1152]{1,0:T(8,128)(2,1)S(1)} %get-tuple-element.67.packed.mine), channel_id=1, source_target_pairs={{0,8},{8,0},{16,24},{24,16},{32,40},{40,32},{48,56},{56,48},{64,72... | collective-permute-start | bytes 10616840 | tf_op jit(solution)/shard_map/ppermute | solution.py:425
  68.8 6.2 %collective-permute-start.11 = (s32[32]{0:T(128)S(1)}, s32[32]{0:T(128)S(1)}, u32[]{:S(2)}, u32[]{:S(2)}) collective-permute-start(s32[32]{0:T(128)S(1)} %get-tuple-element.66.info), channel_id=1, source_target_pairs={{0,8},{8,0},{16,24},{24,16},{32,40},{40,32},{48,56},{56,48},{64,72... | collective-permute-start | bytes 392 | tf_op jit(solution)/shard_map/ppermute | solution.py:424
  71.6 27.2 %copy-start = (bf16[512,1024]{1,0:T(8,128)(2,1)S(1)}, bf16[512,1024]{1,0:T(8,128)(2,1)}, u32[]{:S(2)}) copy-start(bf16[512,1024]{1,0:T(8,128)(2,1)} %embed.1) | copy-start | bytes 3145732
  71.6 27.2 %copy-start.1 = (s32[512,1]{0,1:T(1,128)S(1)}, s32[512,1]{0,1:T(1,128)}, u32[]{:S(2)}) copy-start(s32[512,1]{0,1:T(1,128)} %param.9) | copy-start | bytes 6148
  71.6 27.2 %copy-start.2 = (s32[512]{0:T(512)S(1)}, s32[512]{0:T(512)}, u32[]{:S(2)}) copy-start(s32[512]{0:T(512)} %param.10) | copy-start | bytes 6148
  71.6 27.2 %copy-start.3 = (s32[512]{0:T(512)S(1)}, s32[512]{0:T(512)}, u32[]{:S(2)}) copy-start(s32[512]{0:T(512)} %param.11) | copy-start | bytes 6148
  78.4 18.9 %all-to-all-start.5 = ((f32[64,1,128]{2,1,0:T(1,128)}), f32[64,1,128]{2,1,0:T(1,128)S(1)}, u32[]{:S(2)}, u32[]{:S(2)}) async-start(f32[64,1,128]{2,1,0:T(1,128)} %bitcast.28), calls=%async_computation.5 | async-start | bytes 65536 | tf_op jit(solution)/shard_map/all_to_all | solution.py:358

commit v7 on v6

--- a/solution.py
+++ b/solution.py
@@ -18,6 +18,7 @@
 TILE = 256
 TILES = 6
 PACKED = TILE * TILES
+SIZES = (256, 512, 768, 1024, 1152, 1280, 1408, 1536)
 SPILL = 128
 GROUPS = [[g * 8 + b for g in range(core, 16, 2) for b in range(8)] for core in range(2)]
 COLS = (((1,), (1,)), ((), ()))
@@ -57,7 +58,7 @@
     return turned ^ (((group * 5 + 2) & 15) * 4)
 
 
-def send_kernel(attempt, me, embed, owner, local, rank, out, place, unit, slot, ends):
+def send_kernel(attempt, me, hop, embed, owner, local, rank, out, place, unit, slot, ends):
     rows, width = embed.shape
     step = pl.program_id(0)
     block = out.shape[0]
@@ -70,7 +71,8 @@
         group, number, order = owner[...], local[...], rank[...]
         chip = chip_of(group, number, attempt)
         own = iota((CHIPS, rows), 0) == chip
-        near = iota((CHIPS, rows), 0) == (chip ^ 1)
+        beyond = chip ^ hop[0]
+        near = iota((CHIPS, rows), 0) == beyond
         before = hot(iota((rows, rows), 0) < iota((rows, rows), 1))
         ahead = dot(hot(own), before)
         count = jnp.sum(jnp.where(own, 1.0, 0.0), 1, keepdims=True)
@@ -79,7 +81,7 @@
         spilled = position >= SEATS
         seat = jnp.where(spilled, beside + position - SEATS, position)
         late = jnp.max(jnp.where(seat >= SEATS, 1.0, 0.0), 1, keepdims=True)
-        goes = jnp.where(seat < SEATS, jnp.where(spilled, chip ^ 1, chip), -1)
+        goes = jnp.where(seat < SEATS, jnp.where(spilled, beyond, chip), -1)
         line = seat + jnp.where(spilled, 32, 0)
         slot[...] = jnp.where(goes >= 0, goes * BLOCK + seat, -1)
         place[...] = jnp.where(iota(place.shape, 0) == 0, chip, line)
@@ -170,6 +172,7 @@
     info[16] = (start + TILE - 1) // TILE
     info[17] = jnp.where((start_strange > SPILL) | (late > 0), 1, 0)
     info[18] = start
+    info[19] = start
     pile[...] = jnp.zeros(pile.shape, F32)
 
     @pl.when(start_strange > 0)
@@ -227,6 +230,7 @@
     def _():
         more = (total + count + TILE - 1) // TILE
         info_out[16] = more
+        info_out[19] = total + count
         clear(packed, tiles * (TILE // 16), more * (TILE // 16))
         shift = iota((SPILL + 16, SPILL), 0) - iota((SPILL + 16, SPILL), 1)
         moved = dot(hot(shift == total - begin), near[...])
@@ -235,7 +239,7 @@
         packed[here, :] = jnp.where(keep, packed[here, :].astype(F32), moved).astype(BF16)
 
 
-def score(queries, query_tiles, keys, key_tiles, best, marks, bounds):
+def score(queries, query_rows, keys, key_rows, best, marks, bounds):
     width = queries.shape[1] - EXTRA
     fields = fields_of(queries[:, width:]).astype(I32)
     bounds[0:1, :] = (fields[1:2, :] * 128 + fields[0:1, :] + fields[4:5, :]) * 65536
@@ -249,6 +253,7 @@
         marks[span, :] = jnp.broadcast_to(mark, (TILE, EXTRA))
         return carry
 
+    query_tiles, key_tiles = (query_rows + TILE - 1) // TILE, (key_rows + TILE - 1) // TILE
     lax.fori_loop(0, key_tiles, mark_step, 0)
 
     def against(size):
@@ -264,16 +269,18 @@
 
         lax.fori_loop(0, query_tiles, query_step, 0)
 
-    if isinstance(key_tiles, int):
-        against(key_tiles * TILE)
+    if isinstance(key_rows, int):
+        against(key_rows)
         return
-    for tiles in range(1, keys.shape[0] // TILE + 1):
-        pl.when(key_tiles == tiles)(functools.partial(against, tiles * TILE))
+    low = 0
+    for size in SIZES:
+        pl.when((key_rows > low) & (key_rows <= size))(functools.partial(against, size))
+        low = size
 
 
 def own_kernel(info, packed, best, marks, bounds):
     best[...] = jnp.full(best.shape, -1.0, F32)
-    score(packed, info[16], packed, info[16], best, marks, bounds)
+    score(packed, info[19], packed, info[19], best, marks, bounds)
 
 
 def other_kernel(
@@ -281,7 +288,7 @@
 ):
     best[:, :PACKED] = best_in[...]
     best[:, PACKED:] = jnp.full((1, best.shape[1] - PACKED), -1.0, F32)
-    score(mine, info[16], theirs, other_info[16], best, marks, bounds)
+    score(mine, info[19], theirs, other_info[19], best, marks, bounds)
     flag = jnp.maximum(info[17], other_info[17]).astype(F32)
     reach = 384
     row = iota((16, best.shape[1]), 0)
@@ -365,11 +372,14 @@
     full = width + EXTRA
     lines = CHIPS * BLOCK
     chunks = lines // CHUNK
-    me = ((lax.axis_index("grp") >> 1) * 8 + lax.axis_index("blk")).astype(I32).reshape(1)
+    group = lax.axis_index("grp")
+    core = group & 1
+    me = ((group >> 1) * 8 + lax.axis_index("blk")).astype(I32).reshape(1)
+    hop = (core * 2 + 1).astype(I32).reshape(1)
     sent, place = pl.pallas_call(
         functools.partial(send_kernel, attempt),
         grid=(chunks // 2,),
-        in_specs=[SCALARS, whole((rows, width))] + [whole((1, rows))] * 3,
+        in_specs=[SCALARS, SCALARS, whole((rows, width))] + [whole((1, rows))] * 3,
         out_specs=[pl.BlockSpec((2 * CHUNK, width), lambda i: (i, 0)), whole((8, rows))],
         out_shape=[array((lines, width), BF16), array((8, rows), I32)],
         scratch_shapes=[
@@ -379,7 +389,7 @@
         ],
         compiler_params=LESS,
         name="send",
-    )(me, embed, owner.reshape(1, rows), local_id.reshape(1, rows), rank.reshape(1, rows))
+    )(me, hop, embed, owner.reshape(1, rows), local_id.reshape(1, rows), rank.reshape(1, rows))
     taken = exchange(sent.reshape(CHIPS, BLOCK, width)).reshape(lines, width)
     spill, spots, fields, info = pl.pallas_call(
         read_kernel,
@@ -399,7 +409,8 @@
         compiler_params=LESS,
         name="read",
     )(held(taken))
-    near = lax.ppermute(spill, BOTH, [(i, i ^ 1) for i in range(2 * CHIPS)])
+    beside = [(i, i ^ (1 + (i >> 3 & 1) * 2)) for i in range(2 * CHIPS)]
+    near = lax.ppermute(spill, BOTH, beside)
     packed = pl.pallas_call(
         pack_kernel,
         in_specs=[SCALARS, HELD, HELD, HELD],
@@ -463,8 +474,8 @@
 
 def group_kernel(queries, keys, best_in, best, marks, bounds):
     best[...] = best_in[...]
-    tiles = keys.shape[0] // TILE
-    score(queries, tiles, keys, tiles, best, marks, bounds)
+    rows = keys.shape[0]
+    score(queries, rows, keys, rows, best, marks, bounds)
 
 
 def by_group(embed, owner, local_id, rank):

time: 99.5 us -> 97.2 us (0.977)
  waiting for transfers between devices: 18.1 us -> 15.8 us
    pallas_call x1, Pallas kernels: 3.17 us -> 1.2 us  [direct(): pl.pallas_call(read_kernel, in_specs=[HELD], out_specs=[HELD, HELD, HELD,...]
    pallas_call x1, Pallas kernels: 3.43 us -> 4.89 us  [direct(): pl.pallas_call(other_kernel, in_specs=[SCALARS, SCALARS] + [HELD] * 5, ou...]
    ppermute x1, waiting for transfers between devices: 3.36 us -> 2.17 us  [direct(): other_info = lax.ppermute(info, 'grp', swap)]
    pallas_call x1, Pallas kernels: 2.3 us -> 3.48 us  [direct(): pl.pallas_call(own_kernel, in_specs=[SCALARS, HELD], out_specs=HELD, out_...]
    ppermute x1, waiting for transfers between devices: 5.17 us -> 4.08 us  [direct(): near = lax.ppermute(spill, BOTH, beside)]
    all_to_all x1, starting transfers between devices: 9.39 us -> 8.32 us  [exchange(): lax.all_to_all(x, BOTH, split_axis=0, concat_axis=0, tiled=True, axis_ind...]
  transfers between devices with their start and end apart: 4 -> 4, of which waited for: 3 -> 3; matrix products, arithmetic and copies ran while one was open for 0% -> 0% of each run, Pallas kernels for 4% -> 6%
where the time goes in v7:
time: 97.2 us
  blocking collectives  52.7 us (54%)
  Pallas kernels  18 us (19%)
  waiting for transfers between devices  15.8 us (16%)
  starting transfers between devices  9.55 us (10%)
    all_to_all x1, blocking collectives, exchange(): lax.all_to_all(x, BOTH, split_axis=0, concat_axis=0, tiled=True, axis_ind...  52.7 us
    all_to_all x1, waiting for transfers between devices, exchange(): lax.all_to_all(x, BOTH, split_axis=0, concat_axis=0, tiled=True, axis_ind...  9.55 us
    all_to_all x1, starting transfers between devices, exchange(): lax.all_to_all(x, BOTH, split_axis=0, concat_axis=0, tiled=True, axis_ind...  8.32 us
    pallas_call x1, Pallas kernels, direct(): pl.pallas_call(other_kernel, in_specs=[SCALARS, SCALARS] + [HELD] * 5, ou...  4.89 us
    pallas_call x1, Pallas kernels, direct(): pl.pallas_call(functools.partial(send_kernel, attempt), grid=(chunks // 2...  4.15 us
    ppermute x1, waiting for transfers between devices, direct(): near = lax.ppermute(spill, BOTH, beside)  4.08 us
    pallas_call x1, Pallas kernels, direct(): pl.pallas_call(own_kernel, in_specs=[SCALARS, HELD], out_specs=HELD, out_...  3.48 us
    ppermute x1, waiting for transfers between devices, direct(): other_info = lax.ppermute(info, 'grp', swap)  2.17 us
  transfers between devices with their start and end apart: 4, of which 3 were waited for; matrix products, arithmetic and copies ran while one was open for 0% of the time, Pallas kernels for 6%

profile of v7, /device:TPU:0, one launch (start us, length us, event | category | flops | bytes accessed | tf_op | source)
XLA Modules:
  0.0 97.2 jit_solution(1291629495770727447)
XLA Ops:
  0.0 4.2 %send.3 = (bf16[1536,1024]{1,0:T(8,128)(2,1)S(1)}, s32[8,512]{1,0:T(8,128)S(1)}) custom-call(s32[1]{0:T(128)} %bitcast.22.me, s32[1]{0:T(128)} %bitcast.23.hop, bf16[512,1024]{1,0:T(8,128)(2,1)} %embed.1, s32[1,512]{1,0:T(1,128)} %bitcast.74, s32[1,512]{1,0:T(1,128)} %bitcast.78, s32[1,512]{1,0:T(1,128)} %bitcast.80), custom_call_target="tpu_custom_call" | custom-call | tf_op jit(solution)/shard_map/send/pallas_call | solution.py:379
  4.2 52.7 %all_to_all.41 = bf16[64,24,1024]{2,1,0:T(8,128)(2,1)S(1)} all-to-all(bf16[64,24,1024]{2,1,0:T(8,128)(2,1)S(1)} %bitcast.69), channel_id=1, replica_groups={{0,1,2,3,4,5,6,7,16,17,18,19,20,21,22,23,32,33,34,35,36,37,38,39,48,49,..., dimensions={0} | all-to-all | bytes 6291456 | tf_op jit(solution)/shard_map/all_to_all | solution.py:365
  56.8 1.2 %read.3 = (bf16[128,1152]{1,0:T(8,128)(2,1)S(1)}, s32[8,256]{1,0:T(8,128)S(1)}, bf16[8,128,192]{2,1,0:T(8,128)(2,1)S(1)}, s32[32]{0:T(128)S(1)}) custom-call(bf16[1536,1024]{1,0:T(8,128)(2,1)S(1)} %bitcast.65), custom_call_target="tpu_custom_call" | custom-call | tf_op jit(solution)/shard_map/read/pallas_call | solution.py:394
  58.0 0.6 collective-permute-start.10
  58.7 2.1 %pack.3.packed_in = bf16[1536,1152]{1,0:T(8,128)(2,1)S(1)} custom-call(s32[32]{0:T(128)S(1)} %get-tuple-element.62.info, bf16[1536,1024]{1,0:T(8,128)(2,1)S(1)} %bitcast.66, s32[8,256]{1,0:T(8,128)S(1)} %get-tuple-element.64.spots, bf16[8,128,192]{2,1,0:T(8,128)(2,1)S(1)} %get-tuple-element.65.fields), custom_call_target="tpu_custom_call" | custom-call | flops 736100352 | bytes 7077888 | tf_op jit(solution)/shard_map/pack/pallas_call | solution.py:414
  60.7 4.1 %collective-permute-done.10.near = bf16[128,1152]{1,0:T(8,128)(2,1)S(1)} collective-permute-done((bf16[128,1152]{1,0:T(8,128)(2,1)S(1)}, bf16[128,1152]{1,0:T(8,128)(2,1)S(1)}, u32[]{:S(2)}, u32[]{:S(2)}) %collective-permute-start.10) | collective-permute-done | bytes 294944 | tf_op jit(solution)/shard_map/ppermute | solution.py:413
  64.8 1.3 %append.3 = (bf16[1536,1152]{1,0:T(8,128)(2,1)S(1)}, s32[32]{0:T(128)S(1)}) custom-call(s32[32]{0:T(128)S(1)} %get-tuple-element.62.info, bf16[128,1152]{1,0:T(8,128)(2,1)S(1)} %collective-permute-done.10.near, bf16[1536,1152]{1,0:T(8,128)(2,1)S(1)} %pack.3.packed_in), custom_call_target="tpu_custom_call", output_to_operand_aliasing={{0}: (2, {})} | custom-call | tf_op jit(solution)/shard_map/append/pallas_call | solution.py:425
  66.2 0.1 collective-permute-start.12
  66.3 0.5 collective-permute-start.11
  66.8 3.5 %own.3.best_in = f32[1,1536]{1,0:T(1,128)S(1)} custom-call(s32[32]{0:T(128)S(1)} %get-tuple-element.66.info, bf16[1536,1152]{1,0:T(8,128)(2,1)S(1)} %get-tuple-element.67.packed.mine), custom_call_target="tpu_custom_call" | custom-call | flops 2147483648 | bytes 3538944 | tf_op jit(solution)/shard_map/own/pallas_call | solution.py:437
  70.3 0.0 copy-start
  70.3 0.0 copy-start.1
  70.3 0.0 copy-start.2
  70.3 0.0 copy-start.3
  70.3 2.2 %collective-permute-done.11.other_info = s32[32]{0:T(128)S(1)} collective-permute-done((s32[32]{0:T(128)S(1)}, s32[32]{0:T(128)S(1)}, u32[]{:S(2)}, u32[]{:S(2)}) %collective-permute-start.11) | collective-permute-done | bytes 160 | tf_op jit(solution)/shard_map/ppermute | solution.py:435
  72.5 0.0 collective-permute-done.12.theirs
  72.5 4.9 %other.3 = f32[64,128]{1,0:T(8,128)} custom-call(s32[32]{0:T(128)S(1)} %get-tuple-element.66.info, s32[32]{0:T(128)S(1)} %collective-permute-done.11.other_info, bf16[1536,1152]{1,0:T(8,128)(2,1)S(1)} %get-tuple-element.67.packed.mine, bf16[1536,1152]{1,0:T(8,128)(2,1)S(1)} %collective-permute-done.12.theirs, ...), custom_call_target="tpu_custom_call" | custom-call | tf_op jit(solution)/shard_map/other/pallas_call | solution.py:449
  77.4 8.3 %all-to-all-start.5 = ((f32[64,1,128]{2,1,0:T(1,128)}), f32[64,1,128]{2,1,0:T(1,128)S(1)}, u32[]{:S(2)}, u32[]{:S(2)}) async-start(f32[64,1,128]{2,1,0:T(1,128)} %bitcast.30), calls=%async_computation.5 | async-start | bytes 65536 | tf_op jit(solution)/shard_map/all_to_all | solution.py:365
  85.7 9.6 %all-to-all-done.5 = f32[64,1,128]{2,1,0:T(1,128)S(1)} async-done(((f32[64,1,128]{2,1,0:T(1,128)}), f32[64,1,128]{2,1,0:T(1,128)S(1)}, u32[]{:S(2)}, u32[]{:S(2)}) %all-to-all-start.5) | async-done | bytes 32800 | tf_op jit(solution)/shard_map/all_to_all | solution.py:365
  95.2 0.9 home.3
  96.7 0.0 copy-done
  96.7 0.0 copy-done.1
  96.7 0.0 copy-done.2
  96.7 0.0 copy-done.3
  96.8 0.2 conditional.2
Async XLA Ops:
  58.0 6.8 %collective-permute-start.10 = (bf16[128,1152]{1,0:T(8,128)(2,1)S(1)}, bf16[128,1152]{1,0:T(8,128)(2,1)S(1)}, u32[]{:S(2)}, u32[]{:S(2)}) collective-permute-start(bf16[128,1152]{1,0:T(8,128)(2,1)S(1)} %get-tuple-element.63), channel_id=1, source_target_pairs={{0,1},{1,0},{2,3},{3,2},{4,5},{5,4},{6,7},{7,6},{8,11},{9,10},{10,... | collective-permute-start | bytes 884744 | tf_op jit(solution)/shard_map/ppermute | solution.py:413
  66.2 6.3 %collective-permute-start.12 = (bf16[1536,1152]{1,0:T(8,128)(2,1)S(1)}, bf16[1536,1152]{1,0:T(8,128)(2,1)S(1)}, u32[]{:S(2)}, u32[]{:S(2)}) collective-permute-start(bf16[1536,1152]{1,0:T(8,128)(2,1)S(1)} %get-tuple-element.67.packed.mine), channel_id=1, source_target_pairs={{0,8},{8,0},{16,24},{24,16},{32,40},{40,32},{48,56},{56,48},{64,72... | collective-permute-start | bytes 10616840 | tf_op jit(solution)/shard_map/ppermute | solution.py:436
  66.3 6.2 %collective-permute-start.11 = (s32[32]{0:T(128)S(1)}, s32[32]{0:T(128)S(1)}, u32[]{:S(2)}, u32[]{:S(2)}) collective-permute-start(s32[32]{0:T(128)S(1)} %get-tuple-element.66.info), channel_id=1, source_target_pairs={{0,8},{8,0},{16,24},{24,16},{32,40},{40,32},{48,56},{56,48},{64,72... | collective-permute-start | bytes 392 | tf_op jit(solution)/shard_map/ppermute | solution.py:435
  70.3 26.5 %copy-start = (bf16[512,1024]{1,0:T(8,128)(2,1)S(1)}, bf16[512,1024]{1,0:T(8,128)(2,1)}, u32[]{:S(2)}) copy-start(bf16[512,1024]{1,0:T(8,128)(2,1)} %embed.1) | copy-start | bytes 3145732
  70.3 26.5 %copy-start.1 = (s32[512,1]{0,1:T(1,128)S(1)}, s32[512,1]{0,1:T(1,128)}, u32[]{:S(2)}) copy-start(s32[512,1]{0,1:T(1,128)} %param.9) | copy-start | bytes 6148
  70.3 26.5 %copy-start.2 = (s32[512]{0:T(512)S(1)}, s32[512]{0:T(512)}, u32[]{:S(2)}) copy-start(s32[512]{0:T(512)} %param.10) | copy-start | bytes 6148
  70.3 26.4 %copy-start.3 = (s32[512]{0:T(512)S(1)}, s32[512]{0:T(512)}, u32[]{:S(2)}) copy-start(s32[512]{0:T(512)} %param.11) | copy-start | bytes 6148
  77.4 17.9 %all-to-all-start.5 = ((f32[64,1,128]{2,1,0:T(1,128)}), f32[64,1,128]{2,1,0:T(1,128)S(1)}, u32[]{:S(2)}, u32[]{:S(2)}) async-start(f32[64,1,128]{2,1,0:T(1,128)} %bitcast.30), calls=%async_computation.5 | async-start | bytes 65536 | tf_op jit(solution)/shard_map/all_to_all | solution.py:365
